TPU v7x, 32 devices: a whole 2x2x4 slice. The times are simulated.
32 devices in a mesh: gx: 2 (over y), gy: 4 (over x, core), gz: 4 (over z).
Axes of the slice: x: 2, y: 2, z: 4, core: 2. Of those that a mesh axis runs over, the one named last changes fastest.
Arguments:
- conc: float32 [32, 64, 512], P('gx', 'gy', 'gz'), may hold values from 0 to 1
- right_side: float32 [32, 64, 512], P('gx', 'gy', 'gz'), may hold values from -6144 to 6144
- order_field: bfloat16 [8, 32, 64, 512], P(None, 'gx', 'gy', 'gz'), may hold values from 0 to 1
- grain_ids: int32 [2, 4, 32, 8], P('gx', 'gy', 'gz'), may hold values from 0 to 255, as said below
Outputs:
- solution: float32 [32, 64, 512], P('gx', 'gy', 'gz')
- mobility: float32 [32, 64, 512], P('gx', 'gy', 'gz')
Inputs may be any that keep to these rules, and one draw needn't show every extreme that they name: `grain_ids`: the 8 ids of one block are distinct; neighbouring blocks share some grains, usually in other slots.
All inputs are finite; a program needn't handle non-finite values.
Results may differ from a plain program's by a relative error of at most 0.0019.
Values may be sent and summed in bfloat16 or wider, within the bound.
A program may use at most 128 MiB of HBM per device.

v0:
```python
import jax
import jax.numpy as jnp
from jax import lax
from jax.sharding import PartitionSpec as P

SLOTS = 8
BRICK = 16
SMOOTH = 2
COARSE_SWEEPS = 8


OMEGA = 0.8
TAU_FINE = 256.0


def with_halo(cells, sides, width):
    for axis, dim in sides:
        count = lax.axis_size(axis)
        head = lax.slice_in_dim(cells, 0, width, axis=dim)
        tail = lax.slice_in_dim(cells, cells.shape[dim] - width, cells.shape[dim], axis=dim)
        cells = jnp.concatenate(
            [
                lax.ppermute(tail, axis, [(i, (i + 1) % count) for i in range(count)]),
                cells,
                lax.ppermute(head, axis, [((i + 1) % count, i) for i in range(count)]),
            ],
            axis=dim,
        )
    return cells


def neighbour_view(padded, lead, spatial, direction):
    index = [slice(None)] * lead
    for across in range(3):
        extent = padded.shape[lead + across]
        if across == spatial:
            index.append(slice(1 + direction, extent - 1 + direction))
        else:
            index.append(slice(1, extent - 1))
    return padded[tuple(index)]


def apply_operator(values, padded, coeffs, diag, step):
    summed = None
    for spatial in range(3):
        plus_cell = neighbour_view(padded, 0, spatial, 1)
        minus_cell = neighbour_view(padded, 0, spatial, -1)
        term = coeffs[2 * spatial] * plus_cell + coeffs[2 * spatial + 1] * minus_cell
        summed = term if summed is None else summed + term
    return diag * values - step * summed


def diagonal_of(coeffs, step):
    summed = coeffs[0]
    for coeff in coeffs[1:]:
        summed = summed + coeff
    return 1.0 + step * summed


def jacobi_sweep(values, source, coeffs, diag, step, faces):
    if values is None:
        return OMEGA * source / diag
    padded = faces(values)
    return values + OMEGA * (source - apply_operator(values, padded, coeffs, diag, step)) / diag


def residual_of(values, source, coeffs, diag, step, faces):
    return source - apply_operator(values, faces(values), coeffs, diag, step)


def restrict_field(field):
    extent = field.shape
    grouped = field.reshape(extent[0] // 2, 2, extent[1] // 2, 2, extent[2] // 2, 2)
    return jnp.mean(grouped, axis=(1, 3, 5))


def restrict_coeffs(coeffs):
    result = []
    for position, coeff in enumerate(coeffs):
        spatial = position // 2
        pick = 1 if position % 2 == 0 else 0
        extent = coeff.shape
        grouped = coeff.reshape(extent[0] // 2, 2, extent[1] // 2, 2, extent[2] // 2, 2)
        chosen = jnp.take(grouped, pick, axis=2 * spatial + 1)
        remaining = tuple(
            (
                pair_axis if pair_axis < 2 * spatial + 1 else pair_axis - 1
                for pair_axis in (1, 3, 5)
                if pair_axis != 2 * spatial + 1
            )
        )
        result.append(jnp.mean(chosen, axis=remaining))
    return tuple(result)


def prolong_field(field):
    return jnp.repeat(jnp.repeat(jnp.repeat(field, 2, axis=0), 2, axis=1), 2, axis=2)


def spread_faces(values):
    return with_halo(values, (("gx", 0), ("gy", 1), ("gz", 2)), 1)


def mobility_field(conc, order_field, grain_ids):
    ids_padded = with_halo(grain_ids, (("gx", 0), ("gy", 1), ("gz", 2)), 1)
    own_ids = ids_padded[1:-1, 1:-1, 1:-1]
    order_padded = with_halo(order_field, (("gx", 1), ("gy", 2), ("gz", 3)), 1)
    center = order_padded[:, 1:-1, 1:-1, 1:-1].astype(jnp.float32)
    summed = jnp.zeros(conc.shape, jnp.float32)
    for spatial in range(3):
        for direction in (1, -1):
            edge = BRICK - 1 if direction == 1 else 0
            beside_ids = neighbour_view(ids_padded, 0, spatial, direction)
            matches = (own_ids[..., :, None] == beside_ids[..., None, :]).astype(jnp.float32)
            for across in range(3):
                if across != spatial:
                    matches = jnp.repeat(matches, BRICK, axis=across)
            shifted = neighbour_view(order_padded, 1, spatial, direction).astype(jnp.float32)
            differ = shifted - center
            plain = jnp.sum(differ * differ, axis=0)
            extent = shifted.shape
            split = (
                extent[: spatial + 1]
                + (extent[spatial + 1] // BRICK, BRICK)
                + extent[spatial + 2 :]
            )
            boundary = jnp.take(shifted.reshape(split), edge, axis=spatial + 2)
            center_edge = jnp.take(center.reshape(split), edge, axis=spatial + 2)
            remapped = jnp.zeros(boundary.shape, jnp.float32)
            for other in range(SLOTS):
                remapped = (
                    remapped + jnp.moveaxis(matches[..., other], -1, 0) * boundary[other][None]
                )
            fixed = jnp.sum((remapped - center_edge) ** 2 - (boundary - center_edge) ** 2, axis=0)
            marker = (jnp.arange(BRICK) == edge).reshape((BRICK,) + (1,) * (2 - spatial))
            plain_split = plain.reshape(split[1:])
            plain = jnp.where(
                marker, plain_split + jnp.expand_dims(fixed, spatial + 1), plain_split
            ).reshape(conc.shape)
            summed = summed + plain
    return 1.0 + 8.0 * (conc * (1.0 - conc)) ** 2 + summed


def body(conc, right_side, order_field, grain_ids):
    mobility = mobility_field(conc, order_field, grain_ids)
    step_fine = TAU_FINE
    mobility_padded = with_halo(mobility, (("gx", 0), ("gy", 1), ("gz", 2)), 1)
    coeff_list = []
    for spatial in range(3):
        coeff_list.append(0.5 * (mobility + neighbour_view(mobility_padded, 0, spatial, 1)))
        coeff_list.append(0.5 * (mobility + neighbour_view(mobility_padded, 0, spatial, -1)))
    coeffs_fine = tuple(coeff_list)
    diag_fine = diagonal_of(coeffs_fine, step_fine)
    solution = conc
    for sweep_index in range(SMOOTH):
        solution = jacobi_sweep(
            solution, right_side, coeffs_fine, diag_fine, step_fine, spread_faces
        )
    fine_residual = residual_of(
        solution, right_side, coeffs_fine, diag_fine, step_fine, spread_faces
    )
    source_mid = restrict_field(fine_residual)
    coeffs_mid = restrict_coeffs(coeffs_fine)
    step_mid = TAU_FINE / 4.0
    diag_mid = diagonal_of(coeffs_mid, step_mid)
    error_mid = None
    for sweep_index in range(SMOOTH):
        error_mid = jacobi_sweep(
            error_mid, source_mid, coeffs_mid, diag_mid, step_mid, spread_faces
        )
    mid_residual = residual_of(error_mid, source_mid, coeffs_mid, diag_mid, step_mid, spread_faces)
    source_low = restrict_field(mid_residual)
    coeffs_low = restrict_coeffs(coeffs_mid)
    step_low = TAU_FINE / 16.0
    diag_low = diagonal_of(coeffs_low, step_low)
    error_low = None
    for sweep_index in range(COARSE_SWEEPS):
        error_low = jacobi_sweep(
            error_low, source_low, coeffs_low, diag_low, step_low, spread_faces
        )
    error_mid = error_mid + prolong_field(error_low)
    for sweep_index in range(SMOOTH):
        error_mid = jacobi_sweep(
            error_mid, source_mid, coeffs_mid, diag_mid, step_mid, spread_faces
        )
    solution = solution + prolong_field(error_mid)
    for sweep_index in range(SMOOTH):
        solution = jacobi_sweep(
            solution, right_side, coeffs_fine, diag_fine, step_fine, spread_faces
        )
    return (solution, mobility)


def solution(mesh):
    return jax.shard_map(
        body,
        mesh=mesh,
        in_specs=(
            P("gx", "gy", "gz"),
            P("gx", "gy", "gz"),
            P(None, "gx", "gy", "gz"),
            P("gx", "gy", "gz", None),
        ),
        out_specs=(P("gx", "gy", "gz"), P("gx", "gy", "gz")),
        check_vma=False,
    )
```

profile of v0, /device:TPU:0, one launch (start us, length us, event | category | flops | bytes accessed | tf_op | source)
XLA Modules:
  0.0 494.8 jit_solution(5471889441358015960)
XLA Ops:
  42.6 13.4 %fusion.387 = (f32[8,16,16,8,1]{4,3,2,0,1:T(8,128)}, f32[8,16,16,8,1]{4,3,2,0,1:T(8,128)}) fusion(f32[8,16,16,8,16]{4,3,2,0,1:T(8,128)} %reshape.440), kind=kLoop, calls=%fused_computation.970 | loop fusion | bytes 262144 | tf_op jit(solution)/shard_map/jit(_take) | solution.py:128
  60.0 8.6 %copy.367 = f32[8,16,16,8,1]{2,3,1,0,4:T(8,128)} copy(f32[8,16,16,8,1]{4,3,2,0,1:T(8,128)} %get-tuple-element.239) | data formatting | bytes 131072
  68.5 8.6 %copy.365 = f32[8,16,16,8,1]{2,3,1,0,4:T(8,128)} copy(f32[8,16,16,8,1]{4,3,2,0,1:T(8,128)} %get-tuple-element.240) | data formatting | bytes 131072
  97.3 4.6 reshape.443
  102.0 7.9 %copy.366 = f32[8,16,16,8,1]{2,3,4,1,0:T(8,128)S(1)} copy(f32[8,16,16,8,1]{4,3,2,0,1:T(8,128)} %bitcast.634) | data formatting | bytes 131072
  111.3 4.6 reshape.425
  116.0 9.0 %slice.1912 = f32[8,16,16,8,1]{4,3,2,0,1:T(8,128)} slice(f32[8,16,16,8,16]{4,3,2,0,1:T(8,128)} %reshape.425), slice={[0:8], [0:16], [0:16], [0:8], [15:16]} | slice | bytes 131072 | tf_op jit(solution)/shard_map/jit(_take) | solution.py:127
  125.2 8.0 %copy.364 = f32[8,16,16,8,1]{2,3,4,1,0:T(8,128)S(1)} copy(f32[8,16,16,8,1]{4,3,2,0,1:T(8,128)} %slice.1912) | data formatting | bytes 131072
  150.3 5.2 %collective-permute-done.23 = f32[18,18,1]{2,1,0:T(8,128)S(1)} collective-permute-done((f32[18,18,1]{2,1,0:T(8,128)S(1)}, f32[18,18,1]{2,1,0:T(8,128)S(1)}, u32[]{:S(2)}, u32[]{:S(2)}) %collective-permute-start.23) | collective-permute-done | bytes 1328 | tf_op jit(solution)/shard_map/ppermute | solution.py:23
  159.8 4.7 collective-permute-done.17
  167.7 9.8 %reshape.462 = f32[8,2,8,2,64,2]{5,4,3,2,1,0:T(8,128)} reshape(f32[16,16,128]{2,1,0:T(8,128)S(1)} %get-tuple-element.234) | data formatting | bytes 262144 | tf_op jit(solution)/shard_map/reshape | solution.py:83
  180.3 9.8 %reshape.461 = f32[8,2,8,2,64,2]{5,4,3,2,1,0:T(8,128)} reshape(f32[16,16,128]{2,1,0:T(8,128)S(1)} %get-tuple-element.233) | data formatting | bytes 262144 | tf_op jit(solution)/shard_map/reshape | solution.py:83
  193.5 9.8 %reshape.460 = f32[8,2,8,2,64,2]{5,4,3,2,1,0:T(8,128)} reshape(f32[16,16,128]{2,1,0:T(8,128)S(1)} %get-tuple-element.232) | data formatting | bytes 262144 | tf_op jit(solution)/shard_map/reshape | solution.py:83
  208.5 9.8 %reshape.459 = f32[8,2,8,2,64,2]{5,4,3,2,1,0:T(8,128)} reshape(f32[16,16,128]{2,1,0:T(8,128)S(1)} %get-tuple-element.231) | data formatting | bytes 262144 | tf_op jit(solution)/shard_map/reshape | solution.py:83
  223.5 9.8 %reshape.463 = f32[8,2,8,2,64,2]{5,4,3,2,1,0:T(8,128)} reshape(f32[16,16,128]{2,1,0:T(8,128)S(1)} %get-tuple-element.235) | data formatting | bytes 262144 | tf_op jit(solution)/shard_map/reshape | solution.py:83
  233.3 9.0 %slice.1968 = f32[8,2,8,2,64,1]{5,4,3,2,1,0:T(8,128)} slice(f32[8,2,8,2,64,2]{5,4,3,2,1,0:T(8,128)} %reshape.463), slice={[0:8], [0:2], [0:8], [0:2], [0:64], [1:2]} | slice | bytes 131072 | tf_op jit(solution)/shard_map/jit(_take) | solution.py:84
  242.3 5.4 %copy.353 = f32[8,2,8,2,64,1]{4,2,5,3,1,0:T(8,128)S(1)} copy(f32[8,2,8,2,64,1]{5,4,3,2,1,0:T(8,128)} %slice.1968) | data formatting | bytes 131072 | tf_op jit(solution)/shard_map/jit(_take) | solution.py:84
  248.3 9.8 %reshape.464 = f32[8,2,8,2,64,2]{5,4,3,2,1,0:T(8,128)} reshape(f32[16,16,128]{2,1,0:T(8,128)S(1)} %get-tuple-element.236) | data formatting | bytes 262144 | tf_op jit(solution)/shard_map/reshape | solution.py:83
  258.1 5.4 %copy.354 = f32[8,2,8,2,64,1]{4,2,5,3,1,0:T(8,128)S(1)} copy(f32[8,2,8,2,64,1]{5,4,3,2,1,0:T(8,128)} %bitcast.635) | data formatting | bytes 131072 | tf_op jit(solution)/shard_map/jit(_take) | solution.py:84
  267.5 5.6 %collective-permute-done.34 = f32[18,18,1]{2,1,0:T(8,128)S(1)} collective-permute-done((f32[18,18,1]{2,1,0:T(8,128)S(1)}, f32[18,18,1]{2,1,0:T(8,128)S(1)}, u32[]{:S(2)}, u32[]{:S(2)}) %collective-permute-start.34) | collective-permute-done | bytes 1328 | tf_op jit(solution)/shard_map/ppermute | solution.py:25
  273.0 5.0 %collective-permute-done.35 = f32[18,18,1]{2,1,0:T(8,128)S(1)} collective-permute-done((f32[18,18,1]{2,1,0:T(8,128)S(1)}, f32[18,18,1]{2,1,0:T(8,128)S(1)}, u32[]{:S(2)}, u32[]{:S(2)}) %collective-permute-start.35) | collective-permute-done | bytes 1328 | tf_op jit(solution)/shard_map/ppermute | solution.py:23
  278.2 9.8 %reshape.458 = f32[8,2,8,2,64,2]{5,4,3,2,1,0:T(8,128)} reshape(f32[16,16,128]{2,1,0:T(8,128)S(1)} %fusion.92) | data formatting | bytes 262144 | tf_op jit(solution)/shard_map/reshape | solution.py:73
  463.0 9.8 %collective-permute-done.106 = f32[18,18,1]{2,1,0:T(8,128)S(1)} collective-permute-done((f32[18,18,1]{2,1,0:T(8,128)S(1)}, f32[18,18,1]{2,1,0:T(8,128)S(1)}, u32[]{:S(2)}, u32[]{:S(2)}) %collective-permute-start.106) | collective-permute-done | bytes 1328 | tf_op jit(solution)/shard_map/ppermute | solution.py:25
  483.6 5.7 %collective-permute-done.112 = f32[18,18,1]{2,1,0:T(8,128)S(1)} collective-permute-done((f32[18,18,1]{2,1,0:T(8,128)S(1)}, f32[18,18,1]{2,1,0:T(8,128)S(1)}, u32[]{:S(2)}, u32[]{:S(2)}) %collective-permute-start.112) | collective-permute-done | bytes 1328 | tf_op jit(solution)/shard_map/ppermute | solution.py:25
  (512 shorter events, 303.2 us)
Async XLA Ops:
  4.5 35.8 %collective-permute-start = (bf16[8,1,16,128]{3,2,0,1:T(8,128)(2,1)S(1)}, bf16[8,1,16,128]{3,2,0,1:T(8,128)(2,1)S(1)}, u32[]{:S(2)}, u32[]{:S(2)}) collective-permute-start(bf16[8,1,16,128]{3,2,0,1:T(8,128)(2,1)S(1)} %get-tuple-element.271), channel_id=1, source_target_pairs={{16,0},{0,16},{17,1},{1,17},{18,2},{2,18},{19,3},{3,19},{20,4},{4,... | collective-permute-start | bytes 98312 | tf_op jit(solution)/shard_map/ppermute | solution.py:25
  6.5 26.9 %collective-permute-start.2 = (bf16[8,1,16,128]{3,2,0,1:T(8,128)(2,1)S(1)}, bf16[8,1,16,128]{3,2,0,1:T(8,128)(2,1)S(1)}, u32[]{:S(2)}, u32[]{:S(2)}) collective-permute-start(bf16[8,1,16,128]{3,2,0,1:T(8,128)(2,1)S(1)} %get-tuple-element.272), channel_id=1, source_target_pairs={{0,16},{16,0},{1,17},{17,1},{2,18},{18,2},{3,19},{19,3},{4,20},{20... | collective-permute-start | bytes 98312 | tf_op jit(solution)/shard_map/ppermute | solution.py:23
  7.9 25.5 %collective-permute-start.19 = (f32[1,16,128]{2,1,0:T(8,128)S(1)}, f32[1,16,128]{2,1,0:T(8,128)S(1)}, u32[]{:S(2)}, u32[]{:S(2)}) collective-permute-start(f32[1,16,128]{2,1,0:T(8,128)S(1)} %get-tuple-element.310), channel_id=1, source_target_pairs={{0,16},{16,0},{1,17},{17,1},{2,18},{18,2},{3,19},{19,3},{4,20},{20... | collective-permute-start | bytes 24584 | tf_op jit(solution)/shard_map/ppermute | solution.py:23
  19.3 117.8 %collective-permute-start.18 = (f32[1,16,128]{2,1,0:T(8,128)}, f32[1,16,128]{2,1,0:T(8,128)}, u32[]{:S(2)}, u32[]{:S(2)}) collective-permute-start(f32[1,16,128]{2,1,0:T(8,128)} %get-tuple-element.309), channel_id=1, source_target_pairs={{16,0},{0,16},{17,1},{1,17},{18,2},{2,18},{19,3},{3,19},{20,4},{4,... | collective-permute-start | bytes 24584 | tf_op jit(solution)/shard_map/ppermute | solution.py:25
  40.8 36.4 %collective-permute-start.4 = (bf16[8,18,1,128]{3,2,0,1:T(2,128)(2,1)S(1)}, bf16[8,18,1,128]{3,2,0,1:T(2,128)(2,1)S(1)}, u32[]{:S(2)}, u32[]{:S(2)}) collective-permute-start(bf16[8,18,1,128]{3,2,0,1:T(2,128)(2,1)S(1)} %get-tuple-element.250), channel_id=1, source_target_pairs={{4,0},{8,4},{12,8},{0,12},{5,1},{9,5},{13,9},{1,13},{6,2},{10,6},{... | collective-permute-start | bytes 110600 | tf_op jit(solution)/shard_map/ppermute | solution.py:25
  40.8 36.3 %collective-permute-start.6 = (bf16[8,18,1,128]{3,2,0,1:T(2,128)(2,1)S(1)}, bf16[8,18,1,128]{3,2,0,1:T(2,128)(2,1)S(1)}, u32[]{:S(2)}, u32[]{:S(2)}) collective-permute-start(bf16[8,18,1,128]{3,2,0,1:T(2,128)(2,1)S(1)} %get-tuple-element.249), channel_id=1, source_target_pairs={{0,4},{4,8},{8,12},{12,0},{1,5},{5,9},{9,13},{13,1},{2,6},{6,10},{... | collective-permute-start | bytes 110600 | tf_op jit(solution)/shard_map/ppermute | solution.py:23
  144.4 11.0 %collective-permute-start.23 = (f32[18,18,1]{2,1,0:T(8,128)S(1)}, f32[18,18,1]{2,1,0:T(8,128)S(1)}, u32[]{:S(2)}, u32[]{:S(2)}) collective-permute-start(f32[18,18,1]{2,1,0:T(8,128)S(1)} %get-tuple-element.284), channel_id=1, source_target_pairs={{0,1},{1,2},{2,3},{3,0},{4,5},{5,6},{6,7},{7,4},{8,9},{9,10},{10,1... | collective-permute-start | bytes 3896 | tf_op jit(solution)/shard_map/ppermute | solution.py:23
  144.6 15.2 %collective-permute-start.16 = (f32[18,18,1]{2,1,0:T(8,128)S(1)}, f32[18,18,1]{2,1,0:T(8,128)S(1)}, u32[]{:S(2)}, u32[]{:S(2)}) collective-permute-start(f32[18,18,1]{2,1,0:T(8,128)S(1)} %get-tuple-element.282), channel_id=1, source_target_pairs={{1,0},{2,1},{3,2},{0,3},{5,4},{6,5},{7,6},{4,7},{9,8},{10,9},{11,1... | collective-permute-start | bytes 3896 | tf_op jit(solution)/shard_map/ppermute | solution.py:25
  148.5 16.0 %collective-permute-start.17 = (f32[18,18,1]{2,1,0:T(8,128)S(1)}, f32[18,18,1]{2,1,0:T(8,128)S(1)}, u32[]{:S(2)}, u32[]{:S(2)}) collective-permute-start(f32[18,18,1]{2,1,0:T(8,128)S(1)} %get-tuple-element.281), channel_id=1, source_target_pairs={{0,1},{1,2},{2,3},{3,0},{4,5},{5,6},{6,7},{7,4},{8,9},{9,10},{10,1... | collective-permute-start | bytes 3896 | tf_op jit(solution)/shard_map/ppermute | solution.py:23
  165.6 24.5 %collective-permute-start.24 = (f32[1,16,128]{2,1,0:T(8,128)S(1)}, f32[1,16,128]{2,1,0:T(8,128)S(1)}, u32[]{:S(2)}, u32[]{:S(2)}) collective-permute-start(f32[1,16,128]{2,1,0:T(8,128)S(1)} %get-tuple-element.304), channel_id=1, source_target_pairs={{16,0},{0,16},{17,1},{1,17},{18,2},{2,18},{19,3},{3,19},{20,4},{4,... | collective-permute-start | bytes 24584 | tf_op jit(solution)/shard_map/ppermute | solution.py:25
  166.3 23.8 %collective-permute-start.25 = (f32[1,16,128]{2,1,0:T(8,128)S(1)}, f32[1,16,128]{2,1,0:T(8,128)S(1)}, u32[]{:S(2)}, u32[]{:S(2)}) collective-permute-start(f32[1,16,128]{2,1,0:T(8,128)S(1)} %get-tuple-element.303), channel_id=1, source_target_pairs={{0,16},{16,0},{1,17},{17,1},{2,18},{18,2},{3,19},{19,3},{4,20},{20... | collective-permute-start | bytes 24584 | tf_op jit(solution)/shard_map/ppermute | solution.py:23
  190.1 13.2 %collective-permute-start.26 = (f32[18,1,128]{2,1,0:T(1,128)S(1)}, f32[18,1,128]{2,1,0:T(1,128)S(1)}, u32[]{:S(2)}, u32[]{:S(2)}) collective-permute-start(f32[18,1,128]{2,1,0:T(1,128)S(1)} %get-tuple-element.292), channel_id=1, source_target_pairs={{4,0},{8,4},{12,8},{0,12},{5,1},{9,5},{13,9},{1,13},{6,2},{10,6},{... | collective-permute-start | bytes 27656 | tf_op jit(solution)/shard_map/ppermute | solution.py:25
  190.2 13.1 %collective-permute-start.27 = (f32[18,1,128]{2,1,0:T(1,128)S(1)}, f32[18,1,128]{2,1,0:T(1,128)S(1)}, u32[]{:S(2)}, u32[]{:S(2)}) collective-permute-start(f32[18,1,128]{2,1,0:T(1,128)S(1)} %get-tuple-element.291), channel_id=1, source_target_pairs={{0,4},{4,8},{8,12},{12,0},{1,5},{5,9},{9,13},{13,1},{2,6},{6,10},{... | collective-permute-start | bytes 27656 | tf_op jit(solution)/shard_map/ppermute | solution.py:23
  203.5 14.9 %collective-permute-start.28 = (f32[18,18,1]{2,1,0:T(8,128)S(1)}, f32[18,18,1]{2,1,0:T(8,128)S(1)}, u32[]{:S(2)}, u32[]{:S(2)}) collective-permute-start(f32[18,18,1]{2,1,0:T(8,128)S(1)} %get-tuple-element.279), channel_id=1, source_target_pairs={{1,0},{2,1},{3,2},{0,3},{5,4},{6,5},{7,6},{4,7},{9,8},{10,9},{11,1... | collective-permute-start | bytes 3896 | tf_op jit(solution)/shard_map/ppermute | solution.py:25
  205.3 13.0 %collective-permute-start.29 = (f32[18,18,1]{2,1,0:T(8,128)S(1)}, f32[18,18,1]{2,1,0:T(8,128)S(1)}, u32[]{:S(2)}, u32[]{:S(2)}) collective-permute-start(f32[18,18,1]{2,1,0:T(8,128)S(1)} %get-tuple-element.280), channel_id=1, source_target_pairs={{0,1},{1,2},{2,3},{3,0},{4,5},{5,6},{6,7},{7,4},{8,9},{9,10},{10,1... | collective-permute-start | bytes 3896 | tf_op jit(solution)/shard_map/ppermute | solution.py:23
  218.6 29.1 %collective-permute-start.30 = (f32[1,16,128]{2,1,0:T(8,128)S(1)}, f32[1,16,128]{2,1,0:T(8,128)S(1)}, u32[]{:S(2)}, u32[]{:S(2)}) collective-permute-start(f32[1,16,128]{2,1,0:T(8,128)S(1)} %get-tuple-element.302), channel_id=1, source_target_pairs={{16,0},{0,16},{17,1},{1,17},{18,2},{2,18},{19,3},{3,19},{20,4},{4,... | collective-permute-start | bytes 24584 | tf_op jit(solution)/shard_map/ppermute | solution.py:25
  219.5 28.2 %collective-permute-start.31 = (f32[1,16,128]{2,1,0:T(8,128)S(1)}, f32[1,16,128]{2,1,0:T(8,128)S(1)}, u32[]{:S(2)}, u32[]{:S(2)}) collective-permute-start(f32[1,16,128]{2,1,0:T(8,128)S(1)} %get-tuple-element.301), channel_id=1, source_target_pairs={{0,16},{16,0},{1,17},{17,1},{2,18},{18,2},{3,19},{19,3},{4,20},{20... | collective-permute-start | bytes 24584 | tf_op jit(solution)/shard_map/ppermute | solution.py:23
  247.7 15.8 %collective-permute-start.32 = (f32[18,1,128]{2,1,0:T(1,128)S(1)}, f32[18,1,128]{2,1,0:T(1,128)S(1)}, u32[]{:S(2)}, u32[]{:S(2)}) collective-permute-start(f32[18,1,128]{2,1,0:T(1,128)S(1)} %get-tuple-element.290), channel_id=1, source_target_pairs={{4,0},{8,4},{12,8},{0,12},{5,1},{9,5},{13,9},{1,13},{6,2},{10,6},{... | collective-permute-start | bytes 27656 | tf_op jit(solution)/shard_map/ppermute | solution.py:25
  248.0 15.4 %collective-permute-start.33 = (f32[18,1,128]{2,1,0:T(1,128)S(1)}, f32[18,1,128]{2,1,0:T(1,128)S(1)}, u32[]{:S(2)}, u32[]{:S(2)}) collective-permute-start(f32[18,1,128]{2,1,0:T(1,128)S(1)} %get-tuple-element.289), channel_id=1, source_target_pairs={{0,4},{4,8},{8,12},{12,0},{1,5},{5,9},{9,13},{13,1},{2,6},{6,10},{... | collective-permute-start | bytes 27656 | tf_op jit(solution)/shard_map/ppermute | solution.py:23
  263.7 9.4 %collective-permute-start.34 = (f32[18,18,1]{2,1,0:T(8,128)S(1)}, f32[18,18,1]{2,1,0:T(8,128)S(1)}, u32[]{:S(2)}, u32[]{:S(2)}) collective-permute-start(f32[18,18,1]{2,1,0:T(8,128)S(1)} %get-tuple-element.277), channel_id=1, source_target_pairs={{1,0},{2,1},{3,2},{0,3},{5,4},{6,5},{7,6},{4,7},{9,8},{10,9},{11,1... | collective-permute-start | bytes 3896 | tf_op jit(solution)/shard_map/ppermute | solution.py:25
  267.2 10.8 %collective-permute-start.35 = (f32[18,18,1]{2,1,0:T(8,128)S(1)}, f32[18,18,1]{2,1,0:T(8,128)S(1)}, u32[]{:S(2)}, u32[]{:S(2)}) collective-permute-start(f32[18,18,1]{2,1,0:T(8,128)S(1)} %get-tuple-element.278), channel_id=1, source_target_pairs={{0,1},{1,2},{2,3},{3,0},{4,5},{5,6},{6,7},{7,4},{8,9},{9,10},{10,1... | collective-permute-start | bytes 3896 | tf_op jit(solution)/shard_map/ppermute | solution.py:23
  461.0 11.8 %collective-permute-start.106 = (f32[18,18,1]{2,1,0:T(8,128)S(1)}, f32[18,18,1]{2,1,0:T(8,128)S(1)}, u32[]{:S(2)}, u32[]{:S(2)}) collective-permute-start(f32[18,18,1]{2,1,0:T(8,128)S(1)} %get-tuple-element.275), channel_id=1, source_target_pairs={{1,0},{2,1},{3,2},{0,3},{5,4},{6,5},{7,6},{4,7},{9,8},{10,9},{11,1... | collective-permute-start | bytes 3896 | tf_op jit(solution)/shard_map/ppermute | solution.py:25
  461.7 11.1 %collective-permute-start.107 = (f32[18,18,1]{2,1,0:T(8,128)S(1)}, f32[18,18,1]{2,1,0:T(8,128)S(1)}, u32[]{:S(2)}, u32[]{:S(2)}) collective-permute-start(f32[18,18,1]{2,1,0:T(8,128)S(1)} %get-tuple-element.276), channel_id=1, source_target_pairs={{0,1},{1,2},{2,3},{3,0},{4,5},{5,6},{6,7},{7,4},{8,9},{9,10},{10,1... | collective-permute-start | bytes 3896 | tf_op jit(solution)/shard_map/ppermute | solution.py:23
  482.4 11.1 %collective-permute-start.113 = (f32[18,18,1]{2,1,0:T(8,128)S(1)}, f32[18,18,1]{2,1,0:T(8,128)S(1)}, u32[]{:S(2)}, u32[]{:S(2)}) collective-permute-start(f32[18,18,1]{2,1,0:T(8,128)S(1)} %get-tuple-element.274), channel_id=1, source_target_pairs={{0,1},{1,2},{2,3},{3,0},{4,5},{5,6},{6,7},{7,4},{8,9},{9,10},{10,1... | collective-permute-start | bytes 3896 | tf_op jit(solution)/shard_map/ppermute | solution.py:23
  (127 other events, 785.3 us)
where the time goes:
time: 503 us; the launch traced here: 495 us
  local copies, waits for them, and re-layouts  199 us (40%)
  waiting for transfers between devices  157 us (31%)
  starting transfers between devices  99.2 us (20%)
  other arithmetic  36.5 us (7%)
    ppermute x57, waiting for transfers between devices, with_halo(): lax.ppermute(tail, axis, [(i, (i + 1) % count) for i in range(count)])  80.7 us
    ppermute x57, waiting for transfers between devices, with_halo(): lax.ppermute(head, axis, [((i + 1) % count, i) for i in range(count)])  76.8 us
    reshape x6, local copies, waits for them, and re-layouts, restrict_coeffs(): coeff.reshape(extent[0] // 2, 2, extent[1] // 2, 2, extent[2] // 2, 2)  58.7 us
    ppermute x57, starting transfers between devices, with_halo(): lax.ppermute(tail, axis, [(i, (i + 1) % count) for i in range(count)])  54.1 us
    ppermute x57, starting transfers between devices, with_halo(): lax.ppermute(head, axis, [((i + 1) % count, i) for i in range(count)])  45.1 us
    unnamed x83, local copies, waits for them, and re-layouts  35 us
    another operation x5, local copies, waits for them, and re-layouts, restrict_coeffs(): chosen = jnp.take(grouped, pick, axis=2 * spatial + 1)  20.9 us
    another operation x2, local copies, waits for them, and re-layouts, mobility_field(): center_edge = jnp.take(center.reshape(split), edge, axis=spatial + 2)  14.7 us
  transfers between devices with their start and end apart: 114, of which 85 were waited for; matrix products, arithmetic and copies ran while one was open for 43% of the time, Pallas kernels for 0%

commit v1 on v0

v1 whole, which is shorter than its diff:
```python
import functools

import jax
import jax.numpy as jnp
from jax import lax
from jax.experimental import pallas as pl
from jax.experimental.pallas import tpu as pltpu
from jax.sharding import PartitionSpec as P

SLOTS = 8
BRICK = 16
COARSE_SWEEPS = 8
OMEGA = 0.8
TAU_FINE = 256.0
AXES = ("gx", "gy", "gz")
MESH = pl.DeviceIdType.MESH
HIGHEST = lax.Precision.HIGHEST


def kernel(counts, conc_ref, rhs_ref, order_ref, ids_ref, sol_ref, mob_ref, send, recv, order_y, order_z, order_recv_x,
           order_recv_y, order_recv_z, ids_send, ids_recv, rows_ref, fine_k, coeff0, coeff1, coeff2, send_sem,
           recv_sem, order_send_sem, order_recv_sem, ids_send_sem, ids_recv_sem):
    planes, rows, lanes = conc_ref.shape
    me = tuple(lax.axis_index(axis) for axis in AXES)

    def beside(dim, sign):
        index = list(me)
        index[dim] = lax.rem(me[dim] + sign + counts[dim], counts[dim])
        return tuple(index)

    targets = [beside(dim, sign) for dim in range(3) for sign in (1, -1)]

    barrier = pltpu.get_barrier_semaphore()
    for target in targets:
        pl.semaphore_signal(barrier, inc=1, device_id=target, device_id_type=MESH)
    pl.semaphore_wait(barrier, 6)

    row = lax.broadcasted_iota(jnp.int32, (rows, lanes), 0)
    lane = lax.broadcasted_iota(jnp.int32, (rows, lanes), 1)
    zero = jnp.zeros((rows, lanes), jnp.float32)
    started = []

    def start(source, dest, source_sem, dest_sem, face):
        copy = pltpu.make_async_remote_copy(
            src_ref=source, dst_ref=dest, send_sem=source_sem, recv_sem=dest_sem, device_id=targets[face],
            device_id_type=MESH)
        copy.start()
        started.append(copy)
        return copy

    def spread_row(line):
        return jnp.broadcast_to(line, (rows, lanes))

    def spread_lane(column):
        return jnp.broadcast_to(column, (rows, lanes))

    def send_faces(turn, field):
        count = len(field)
        copies = []

        def go(face, extent):
            copies.append(start(
                send.at[turn, face, pl.ds(0, extent)], recv.at[turn, face, pl.ds(0, extent)],
                send_sem.at[turn, face], recv_sem.at[turn, face], face))

        send[turn, 0] = field[-1]
        go(0, rows)
        send[turn, 1] = field[0]
        go(1, rows)
        extent = max(count, 8)
        for face, at in ((2, rows - 1), (3, 0)):
            for i in range(extent):
                send[turn, face, i:i + 1, :] = field[i % count][at:at + 1, :]
            go(face, extent)
        for face, at in ((4, lanes - 1), (5, 0)):
            packed = zero
            for i in range(count):
                packed = jnp.where(lane == i, spread_lane(field[i][:, at:at + 1]), packed)
            send[turn, face] = packed
            go(face, rows)
        return copies

    def edge_rows(turn, i):
        return jnp.where(row < rows // 2, spread_row(recv[turn, 2, i:i + 1, :]), spread_row(recv[turn, 3, i:i + 1, :]))

    def edge_lanes(minus, plus, i):
        return jnp.where(lane < lanes // 2, spread_lane(minus[:, i:i + 1]), spread_lane(plus[:, i:i + 1]))

    def wait(copies):
        for copy in copies:
            copy.wait_recv()

    ids = ids_ref[0, 0].astype(jnp.float32)
    blocks = ids.shape[0]
    shape = (blocks, lanes)
    chosen = (lax.broadcasted_iota(jnp.int32, shape, 1) // BRICK == lax.broadcasted_iota(jnp.int32, shape, 0))
    chosen = chosen.astype(jnp.float32)
    ids_lane = lax.dot_general(ids, chosen, (((0,), (0,)), ((), ())), precision=HIGHEST,
                               preferred_element_type=jnp.float32)
    ids_slot = lax.dot_general(ids, chosen, (((1,), (0,)), ((), ())), precision=HIGHEST,
                               preferred_element_type=jnp.float32)
    ids_send[0] = ids_lane
    ids_send[1] = ids_slot
    ids_copies = [
        start(ids_send.at[face // 4], ids_recv.at[face], ids_send_sem.at[face], ids_recv_sem.at[face], face)
        for face in range(6)
    ]
    order_copies = [
        start(order_ref.at[:, planes - 1], order_recv_x.at[0], order_send_sem.at[0], order_recv_sem.at[0], 0),
        start(order_ref.at[:, 0], order_recv_x.at[1], order_send_sem.at[1], order_recv_sem.at[1], 1),
    ]

    def pack(i, carry):
        last, first = carry
        for s in range(SLOTS):
            plane = order_ref[s, i].astype(jnp.float32)
            rows_ref[0, s, pl.ds(i, 1), :] = plane[rows - 1:rows, :]
            rows_ref[1, s, pl.ds(i, 1), :] = plane[0:1, :]
            here = lane == s * BRICK + i
            last = jnp.where(here, spread_lane(plane[:, lanes - 1:lanes]), last)
            first = jnp.where(here, spread_lane(plane[:, 0:1]), first)
        return last, first

    last, first = lax.fori_loop(0, planes, pack, (zero, zero))
    for face in range(2):
        order_y[face] = rows_ref[face].astype(jnp.bfloat16)
        order_copies.append(start(order_y.at[face], order_recv_y.at[face], order_send_sem.at[2 + face],
                                  order_recv_sem.at[2 + face], 2 + face))
    for face, value in ((0, last), (1, first)):
        order_z[face] = value.astype(jnp.bfloat16)
        order_copies.append(start(order_z.at[face], order_recv_z.at[face], order_send_sem.at[4 + face],
                                  order_recv_sem.at[4 + face], 4 + face))
    conc = [conc_ref[i] for i in range(planes)]
    conc_copies = send_faces(0, conc)

    id_lane = lax.broadcasted_iota(jnp.int32, shape, 1)
    ids_next = jnp.where(id_lane == lanes - 1, -1.0, pltpu.roll(ids_lane, lanes - 1, 1))
    ids_before = jnp.where(id_lane == 0, -1.0, pltpu.roll(ids_lane, 1, 1))
    matched, alone = [], []
    for s in range(SLOTS):
        own = jnp.broadcast_to(ids_lane[s:s + 1, :], shape)
        hit = jnp.sum((own == ids_next).astype(jnp.float32), axis=0, keepdims=True)
        matched.append(hit)
        hit = jnp.sum((own == ids_before).astype(jnp.float32), axis=0, keepdims=True)
        alone.append(jnp.where(lax.broadcasted_iota(jnp.int32, (1, lanes), 1) == 0, 0.0, 1.0 - hit))

    def remap(own_ids, other_ids, others):
        result = []
        for s in range(SLOTS):
            value = zero
            for t in range(SLOTS):
                value = jnp.where(spread_row(own_ids[s:s + 1, :]) == spread_row(other_ids[t:t + 1, :]), others[t], value)
            result.append(value)
        return result

    def inside(i, carry):
        above = jnp.minimum(i + 1, planes - 1)
        below = jnp.maximum(i - 1, 0)
        own = [order_ref[s, i].astype(jnp.float32) for s in range(SLOTS)]
        rolled = [pltpu.roll(plane, lanes - 1, 1) for plane in own]
        mapped = remap(ids_lane, ids_next, rolled)
        c = conc_ref[i]
        reaction = c * (1.0 - c)
        total = 1.0 + 8.0 * (reaction * reaction)
        along_y, along_z, shared = zero, zero, zero
        for s in range(SLOTS):
            differ = order_ref[s, above].astype(jnp.float32) - own[s]
            total = total + differ * differ
            differ = order_ref[s, below].astype(jnp.float32) - own[s]
            total = total + differ * differ
            differ = pltpu.roll(own[s], rows - 1, 0) - own[s]
            along_y = along_y + differ * differ
            differ = mapped[s] - own[s]
            square = differ * differ
            along_z = along_z + square
            shared = shared + matched[s] * square
            total = total + alone[s] * (own[s] * own[s])
        along_y = jnp.where(row == rows - 1, 0.0, along_y)
        along_z = jnp.where(lane == lanes - 1, 0.0, along_z)
        total = total + along_y + pltpu.roll(along_y, 1, 0)
        total = total + along_z + pltpu.roll(shared, 1, 1)
        mob_ref[i] = total
        return carry

    lax.fori_loop(0, planes, inside, 0)

    wait(ids_copies)
    wait(order_copies)
    for face, at in ((1, planes - 1), (0, 0)):
        others = [order_recv_x[face, t].astype(jnp.float32) for t in range(SLOTS)]
        mapped = remap(ids_lane, ids_recv[face], others)
        total = mob_ref[at]
        for s in range(SLOTS):
            differ = mapped[s] - order_ref[s, at].astype(jnp.float32)
            total = total + differ * differ
        mob_ref[at] = total
    across = []
    for face in (0, 1):
        others = [order_recv_y[face, t].astype(jnp.float32) for t in range(SLOTS)]
        mapped = remap(ids_lane, ids_recv[2 + face], others)
        total = zero
        for s in range(SLOTS):
            differ = mapped[s] - rows_ref[1 - face, s]
            total = total + differ * differ
        across.append(total)
    ends = []
    for face, own, block in ((0, first, 0), (1, last, blocks - 1)):
        own_ids = spread_row(ids_slot[block:block + 1, :])
        other_block = blocks - 1 - block
        other_ids = spread_row(ids_recv[4 + face, other_block:other_block + 1, :])
        others = order_recv_z[face].astype(jnp.float32)
        value = zero
        for shift in range(0, lanes, BRICK):
            same = own_ids == (pltpu.roll(other_ids, shift, 1) if shift else other_ids)
            value = jnp.where(same, pltpu.roll(others, shift, 1) if shift else others, value)
        differ = value - own
        total = differ * differ
        for shift in (64, 32, 16):
            total = total + pltpu.roll(total, shift, 1)
        ends.append(total)
    mobility = []
    for i in range(planes):
        total = mob_ref[i]
        total = total + jnp.where(row == 0, spread_row(across[0][i:i + 1, :]), 0.0)
        total = total + jnp.where(row == rows - 1, spread_row(across[1][i:i + 1, :]), 0.0)
        at_edge = jnp.logical_or(lane == 0, lane == lanes - 1)
        total = total + jnp.where(at_edge, edge_lanes(ends[0], ends[1], i), 0.0)
        mob_ref[i] = total
        mobility.append(total)
    copies = send_faces(1, mobility)
    wait(copies)

    minus, plus = recv[1, 4], recv[1, 5]
    for i in range(planes):
        own = mobility[i]
        rims = edge_rows(1, i)
        tips = edge_lanes(minus, plus, i)
        fine_k[0, i] = 0.5 * (own + (mobility[i + 1] if i < planes - 1 else recv[1, 1]))
        fine_k[1, i] = 0.5 * (own + (mobility[i - 1] if i > 0 else recv[1, 0]))
        fine_k[2, i] = 0.5 * (own + jnp.where(row == rows - 1, rims, pltpu.roll(own, rows - 1, 0)))
        fine_k[3, i] = 0.5 * (own + jnp.where(row == 0, rims, pltpu.roll(own, 1, 0)))
        fine_k[4, i] = 0.5 * (own + jnp.where(lane == lanes - 1, tips, pltpu.roll(own, lanes - 1, 1)))
        fine_k[5, i] = 0.5 * (own + jnp.where(lane == 0, tips, pltpu.roll(own, 1, 1)))

    def build(store, faces, tau, width):
        for i in range(len(faces[0])):
            k = [face[i] for face in faces]
            diag = 1.0 + tau * (k[0] + k[1] + k[2] + k[3] + k[4] + k[5])
            weight = OMEGA / diag
            scale = tau * weight
            store[0, i] = scale * k[0]
            store[1, i] = scale * k[1]
            top, bottom = row >= rows - width, row < width
            right, left = lane >= lanes - width, lane < width
            a, b = scale * k[2], scale * k[3]
            store[2, i] = jnp.where(top, 0.0, a)
            store[3, i] = jnp.where(bottom, 0.0, b)
            store[4, i] = jnp.where(top, a, jnp.where(bottom, b, 0.0))
            a, b = scale * k[4], scale * k[5]
            store[5, i] = jnp.where(right, 0.0, a)
            store[6, i] = jnp.where(left, 0.0, b)
            store[7, i] = jnp.where(right, a, jnp.where(left, b, 0.0))
            store[8, i] = weight
            store[9, i] = diag * (1.0 / OMEGA)

    def swap(value, dim, width):
        size = value.shape[dim]
        index = row if dim == 0 else lane
        upper = (index // width) % 2 == 1
        return upper, pltpu.roll(value, width, dim), pltpu.roll(value, size - width, dim)

    def mean_pair(value, dim, width):
        upper, down, up = swap(value, dim, width)
        return 0.5 * (value + jnp.where(upper, down, up))

    def take_upper(value, dim, width):
        upper, _, up = swap(value, dim, width)
        return jnp.where(upper, value, up)

    def take_lower(value, dim, width):
        upper, down, _ = swap(value, dim, width)
        return jnp.where(upper, down, value)

    def coarsen(faces, width):
        result = [[] for _ in range(6)]
        for i in range(len(faces[0]) // 2):
            def both(face):
                return 0.5 * (faces[face][2 * i] + faces[face][2 * i + 1])
            result[0].append(mean_pair(mean_pair(faces[0][2 * i + 1], 0, width), 1, width))
            result[1].append(mean_pair(mean_pair(faces[1][2 * i], 0, width), 1, width))
            result[2].append(mean_pair(take_upper(both(2), 0, width), 1, width))
            result[3].append(mean_pair(take_lower(both(3), 0, width), 1, width))
            result[4].append(mean_pair(take_upper(both(4), 1, width), 0, width))
            result[5].append(mean_pair(take_lower(both(5), 1, width), 0, width))
        return result

    def restrict(field, width):
        return [
            mean_pair(mean_pair(0.5 * (field[2 * i] + field[2 * i + 1]), 0, width), 1, width)
            for i in range(len(field) // 2)
        ]

    def sweep(turn, field, weighted, store, width, copies, keep, between=None):
        count = len(field)
        totals = []
        for i in range(count):
            own = field[i]
            total = keep * own + weighted[i]
            if i < count - 1:
                total = total + store[0, i] * field[i + 1]
            if i > 0:
                total = total + store[1, i] * field[i - 1]
            total = total + store[2, i] * pltpu.roll(own, rows - width, 0)
            total = total + store[3, i] * pltpu.roll(own, width, 0)
            total = total + store[5, i] * pltpu.roll(own, lanes - width, 1)
            total = total + store[6, i] * pltpu.roll(own, width, 1)
            totals.append(total)
        if between is not None:
            between()
        wait(copies)
        minus, plus = recv[turn, 4], recv[turn, 5]
        for i in range(count):
            total = totals[i] + store[4, i] * edge_rows(turn, i) + store[7, i] * edge_lanes(minus, plus, i)
            if i == count - 1:
                total = total + store[0, i] * recv[turn, 1]
            if i == 0:
                total = total + store[1, i] * recv[turn, 0]
            totals[i] = total
        return totals

    faces0 = [[fine_k[face, i] for i in range(planes)] for face in range(6)]
    build(coeff0, faces0, TAU_FINE, 1)
    weighted0 = [coeff0[8, i] * rhs_ref[i] for i in range(planes)]
    keep = 1.0 - OMEGA
    field = sweep(0, conc, weighted0, coeff0, 1, conc_copies, keep)

    faces1 = []

    def build_middle():
        faces1.extend(coarsen(faces0, 1))
        build(coeff1, faces1, TAU_FINE / 4.0, 2)

    copies = send_faces(2, field)
    field = sweep(2, field, weighted0, coeff0, 1, copies, keep, build_middle)

    def build_low():
        build(coeff2, coarsen(faces1, 2), TAU_FINE / 16.0, 4)

    copies = send_faces(3, field)
    added = sweep(3, field, weighted0, coeff0, 1, copies, -OMEGA, build_low)
    source1 = restrict([added[i] * coeff0[9, i] for i in range(planes)], 1)
    middle = planes // 2
    weighted1 = [coeff1[8, i] * source1[i] for i in range(middle)]
    error1 = weighted1
    copies = send_faces(4, error1)
    error1 = sweep(4, error1, weighted1, coeff1, 2, copies, keep)
    copies = send_faces(5, error1)
    added = sweep(5, error1, weighted1, coeff1, 2, copies, -OMEGA)
    source2 = restrict([added[i] * coeff1[9, i] for i in range(middle)], 2)
    low = planes // 4
    weighted2 = [coeff2[8, i] * source2[i] for i in range(low)]
    error2 = weighted2
    turn = 6
    for _ in range(COARSE_SWEEPS - 1):
        copies = send_faces(turn, error2)
        error2 = sweep(turn, error2, weighted2, coeff2, 4, copies, keep)
        turn += 1
    error1 = [error1[i] + error2[i // 2] for i in range(middle)]
    for _ in range(2):
        copies = send_faces(turn, error1)
        error1 = sweep(turn, error1, weighted1, coeff1, 2, copies, keep)
        turn += 1
    field = [field[i] + error1[i // 2] for i in range(planes)]
    for _ in range(2):
        copies = send_faces(turn, field)
        field = sweep(turn, field, weighted0, coeff0, 1, copies, keep)
        turn += 1
    for i in range(planes):
        sol_ref[i] = field[i]
    for copy in started:
        copy.wait_send()


TURNS = 6 + (COARSE_SWEEPS - 1) + 4


def body(counts, conc, right_side, order_field, grain_ids):
    planes, rows, lanes = conc.shape
    blocks = grain_ids.shape[2]
    vmem = pl.BlockSpec(memory_space=pltpu.VMEM)
    f32, bf16 = jnp.float32, jnp.bfloat16
    dma = pltpu.SemaphoreType.DMA
    out = jax.ShapeDtypeStruct(conc.shape, f32)
    return pl.pallas_call(
        functools.partial(kernel, counts),
        out_shape=(out, out),
        in_specs=[vmem] * 4,
        out_specs=(vmem, vmem),
        scratch_shapes=[
            pltpu.VMEM((TURNS, 6, rows, lanes), f32),
            pltpu.VMEM((TURNS, 6, rows, lanes), f32),
            pltpu.VMEM((2, SLOTS, planes, lanes), bf16),
            pltpu.VMEM((2, rows, lanes), bf16),
            pltpu.VMEM((2, SLOTS, rows, lanes), bf16),
            pltpu.VMEM((2, SLOTS, planes, lanes), bf16),
            pltpu.VMEM((2, rows, lanes), bf16),
            pltpu.VMEM((2, blocks, lanes), f32),
            pltpu.VMEM((6, blocks, lanes), f32),
            pltpu.VMEM((2, SLOTS, planes, lanes), f32),
            pltpu.VMEM((6, planes, rows, lanes), f32),
            pltpu.VMEM((10, planes, rows, lanes), f32),
            pltpu.VMEM((10, planes // 2, rows, lanes), f32),
            pltpu.VMEM((10, planes // 4, rows, lanes), f32),
            dma((TURNS, 6)),
            dma((TURNS, 6)),
            dma((6,)),
            dma((6,)),
            dma((6,)),
            dma((6,)),
        ],
        compiler_params=pltpu.CompilerParams(
            collective_id=0, has_side_effects=True, vmem_limit_bytes=40 * 1024 * 1024
        ),
    )(conc, right_side, order_field, grain_ids)


def solution(mesh):
    counts = tuple(mesh.shape[axis] for axis in AXES)
    return jax.shard_map(
        functools.partial(body, counts),
        mesh=mesh,
        in_specs=(
            P("gx", "gy", "gz"),
            P("gx", "gy", "gz"),
            P(None, "gx", "gy", "gz"),
            P("gx", "gy", "gz", None),
        ),
        out_specs=(P("gx", "gy", "gz"), P("gx", "gy", "gz")),
        check_vma=False,
    )
```

time: 503 us -> 79.5 us (0.16); the launches traced: 495 us -> 79.2 us
  local copies, waits for them, and re-layouts: 199 us -> 4.84 us
  waiting for transfers between devices: 157 us -> 0 us
  starting transfers between devices: 99.2 us -> 0 us
  Pallas kernels: 0 us -> 73.7 us
  other arithmetic: 36.5 us -> 0 us
    ppermute x114 -> x0, waiting for transfers between devices: 157 us -> none  [the longest x57 80.7 us: with_halo(): lax.ppermute(tail, axis, [(i, (i + 1) % count) for i in range(count)])]
    ppermute x114 -> x0, starting transfers between devices: 99.2 us -> none  [the longest x57 54.1 us: with_halo(): lax.ppermute(tail, axis, [(i, (i + 1) % count) for i in range(count)])]
    reshape x32 -> x0, local copies, waits for them, and re-layouts: 94.4 us -> none  [the longest x6 58.7 us: restrict_coeffs(): coeff.reshape(extent[0] // 2, 2, extent[1] // 2, 2, extent[2] // 2, 2)]
    pallas_call x0 -> x1, Pallas kernels: none -> 73.7 us  [body(): pl.pallas_call(functools.partial(kernel, counts), out_shape=(out, out), i...]
    another operation x10 -> x0, local copies, waits for them, and re-layouts: 44.7 us -> none  [the longest x5 20.9 us: restrict_coeffs(): chosen = jnp.take(grouped, pick, axis=2 * spatial + 1)]
    unnamed x83 -> x10, local copies, waits for them, and re-layouts: 35 us -> 4.84 us
    reduce_sum x22 -> x0, other arithmetic: 28.3 us -> none  [the longest x12 12 us: restrict_coeffs(): result.append(jnp.mean(chosen, axis=remaining))]
    slice x46 -> x0, local copies, waits for them, and re-layouts: 8.15 us -> none  [the longest x19 4.47 us: with_halo(): head = lax.slice_in_dim(cells, 0, width, axis=dim)]
  transfers between devices with their start and end apart: 114 -> 0, of which waited for: 85 -> 0; matrix products, arithmetic and copies ran while one was open for 43% -> 0% of each run, Pallas kernels for 0% -> 0%
where the time goes in v1:
time: 79.5 us; the launch traced here: 79.2 us
  Pallas kernels  73.7 us (93%)
  local copies, waits for them, and re-layouts  4.84 us (6%)
    pallas_call x1, Pallas kernels, body(): pl.pallas_call(functools.partial(kernel, counts), out_shape=(out, out), i...  73.7 us
    unnamed x10, local copies, waits for them, and re-layouts  4.84 us

profile of v1, /device:TPU:0, one launch (start us, length us, event | category | flops | bytes accessed | tf_op | source)
XLA Modules:
  0.0 79.2 jit_solution(4610881092705207756)
XLA Ops:
  0.6 0.0 copy-start
  0.6 1.0 %copy-done = bf16[8,16,16,128]{3,2,1,0:T(8,128)(2,1)S(1)} copy-done((bf16[8,16,16,128]{3,2,1,0:T(8,128)(2,1)S(1)}, bf16[8,16,16,128]{3,2,1,0:T(8,128)(2,1)}, u32[]{:S(2)}) %copy-start) | copy-done | bytes 524312
  1.7 0.0 copy-start.1
  1.7 0.9 %copy-done.1 = f32[16,16,128]{2,1,0:T(8,128)S(1)} copy-done((f32[16,16,128]{2,1,0:T(8,128)S(1)}, f32[16,16,128]{2,1,0:T(8,128)}, u32[]{:S(2)}) %copy-start.1) | copy-done | bytes 131096
  2.6 0.0 copy-start.2
  2.6 0.9 %copy-done.2 = f32[16,16,128]{2,1,0:T(8,128)S(1)} copy-done((f32[16,16,128]{2,1,0:T(8,128)S(1)}, f32[16,16,128]{2,1,0:T(8,128)}, u32[]{:S(2)}) %copy-start.2) | copy-done | bytes 131096
  3.5 0.0 copy-start.3
  3.5 0.7 copy-done.3
  4.2 73.7 %shard_map.59 = (f32[16,16,128]{2,1,0:T(8,128)S(1)}, f32[16,16,128]{2,1,0:T(8,128)S(1)}) custom-call(f32[16,16,128]{2,1,0:T(8,128)S(1)} %copy-done.1, f32[16,16,128]{2,1,0:T(8,128)S(1)} %copy-done.2, bf16[8,16,16,128]{3,2,1,0:T(8,128)(2,1)S(1)} %copy-done, s32[1,1,8,8]{3,2,1,0:T(8,128)S(1)} %copy-done.3), custom_call_target="tpu_custom_call" | custom-call | tf_op jit(solution)/shard_map/pallas_call | solution.py:394
  77.9 0.7 copy.8
  78.6 0.7 copy.9
Async XLA Ops:
  0.6 1.0 %copy-start = (bf16[8,16,16,128]{3,2,1,0:T(8,128)(2,1)S(1)}, bf16[8,16,16,128]{3,2,1,0:T(8,128)(2,1)}, u32[]{:S(2)}) copy-start(bf16[8,16,16,128]{3,2,1,0:T(8,128)(2,1)} %order_ref.1) | copy-start | bytes 1572868
  1.7 0.9 %copy-start.1 = (f32[16,16,128]{2,1,0:T(8,128)S(1)}, f32[16,16,128]{2,1,0:T(8,128)}, u32[]{:S(2)}) copy-start(f32[16,16,128]{2,1,0:T(8,128)} %conc_ref.1) | copy-start | bytes 393220
  2.6 0.9 %copy-start.2 = (f32[16,16,128]{2,1,0:T(8,128)S(1)}, f32[16,16,128]{2,1,0:T(8,128)}, u32[]{:S(2)}) copy-start(f32[16,16,128]{2,1,0:T(8,128)} %rhs_ref.1) | copy-start | bytes 393220
  3.5 0.7 copy-start.3

commit v2 on v1

--- a/solution.py
+++ b/solution.py
@@ -17,10 +17,20 @@
 HIGHEST = lax.Precision.HIGHEST
 
 
-def kernel(counts, conc_ref, rhs_ref, order_ref, ids_ref, sol_ref, mob_ref, send, recv, order_y, order_z, order_recv_x,
+def kernel(counts, conc_in, rhs_in, order_in, ids_in, sol_ref, mob_ref, conc_ref, rhs_ref, order_ref, ids_ref, rhs_wide,
+           deep_send, deep_recv, send, recv, order_y, order_z, order_recv_x,
            order_recv_y, order_recv_z, ids_send, ids_recv, rows_ref, fine_k, coeff0, coeff1, coeff2, send_sem,
-           recv_sem, order_send_sem, order_recv_sem, ids_send_sem, ids_recv_sem):
+           recv_sem, order_send_sem, order_recv_sem, ids_send_sem, ids_recv_sem, deep_send_sem, deep_recv_sem, load_sem):
     planes, rows, lanes = conc_ref.shape
+    wide = 2 * lanes
+    half = lanes // 2
+    loads = [
+        pltpu.make_async_copy(source, dest, load_sem.at[position])
+        for position, (source, dest) in enumerate(
+            ((ids_in, ids_ref), (order_in, order_ref), (conc_in, conc_ref), (rhs_in, rhs_ref)))
+    ]
+    for load in loads:
+        load.start()
     me = tuple(lax.axis_index(axis) for axis in AXES)
 
     def beside(dim, sign):
@@ -34,6 +44,8 @@
     for target in targets:
         pl.semaphore_signal(barrier, inc=1, device_id=target, device_id_type=MESH)
     pl.semaphore_wait(barrier, 6)
+    for load in loads:
+        load.wait()
 
     row = lax.broadcasted_iota(jnp.int32, (rows, lanes), 0)
     lane = lax.broadcasted_iota(jnp.int32, (rows, lanes), 1)
@@ -54,34 +66,75 @@
     def spread_lane(column):
         return jnp.broadcast_to(column, (rows, lanes))
 
-    def send_faces(turn, field):
+    wide_row = lax.broadcasted_iota(jnp.int32, (rows, wide), 0)
+    wide_lane = lax.broadcasted_iota(jnp.int32, (rows, wide), 1)
+
+    def fold(face, width):
+        if width == 1:
+            return face
+        parity = lax.broadcasted_iota(jnp.int32, (face.shape[0], lanes), 1) % 2
+        return jnp.where(parity == 0, face[:, :lanes], face[:, lanes:])
+
+    def unfold(face, width):
+        if width == 1:
+            return face
+        parity = lax.broadcasted_iota(jnp.int32, face.shape, 1) % 2
+        own = jnp.where(parity == 0, face, pltpu.roll(face, 1, 1))
+        other = jnp.where(parity == 0, pltpu.roll(face, lanes - 1, 1), face)
+        return jnp.concatenate([own, other], axis=1)
+
+    def send_faces(turn, field, width):
         count = len(field)
+        extent = max(count, 8)
+        span = pl.ds(0, wide if width == 1 else lanes)
         copies = []
 
         def go(face, extent):
-            copies.append(start(
-                send.at[turn, face, pl.ds(0, extent)], recv.at[turn, face, pl.ds(0, extent)],
-                send_sem.at[turn, face], recv_sem.at[turn, face], face))
-
-        send[turn, 0] = field[-1]
+            part = (turn, face, pl.ds(0, extent), span)
+            copies.append(start(send.at[part], recv.at[part], send_sem.at[turn, face], recv_sem.at[turn, face], face))
+
+        send[turn, 0, :, span] = fold(field[-1], width)
         go(0, rows)
-        send[turn, 1] = field[0]
+        send[turn, 1, :, span] = fold(field[0], width)
         go(1, rows)
-        extent = max(count, 8)
         for face, at in ((2, rows - 1), (3, 0)):
             for i in range(extent):
-                send[turn, face, i:i + 1, :] = field[i % count][at:at + 1, :]
+                send[turn, face, i:i + 1, span] = fold(field[i % count][at:at + 1, :], width)
             go(face, extent)
-        for face, at in ((4, lanes - 1), (5, 0)):
-            packed = zero
-            for i in range(count):
-                packed = jnp.where(lane == i, spread_lane(field[i][:, at:at + 1]), packed)
-            send[turn, face] = packed
-            go(face, rows)
         return copies
 
-    def edge_rows(turn, i):
-        return jnp.where(row < rows // 2, spread_row(recv[turn, 2, i:i + 1, :]), spread_row(recv[turn, 3, i:i + 1, :]))
+    def get_faces(turn, count, width):
+        extent = max(count, 8)
+        span = pl.ds(0, wide if width == 1 else lanes)
+        return [unfold(recv[turn, face, pl.ds(0, rows if face < 2 else extent), span], width) for face in range(4)]
+
+    def edge_rows(faces, i):
+        return jnp.where(wide_row < rows // 2, jnp.broadcast_to(faces[2][i:i + 1, :], (rows, wide)),
+                         jnp.broadcast_to(faces[3][i:i + 1, :], (rows, wide)))
+
+    def send_halves(kind, firsts, seconds):
+        copies = []
+        for face in range(2):
+            for i in range(len(firsts)):
+                if face == 0:
+                    value = jnp.where(lane < half, pltpu.roll(firsts[i], half, 1), seconds[i])
+                else:
+                    value = jnp.where(lane < half, firsts[i], pltpu.roll(seconds[i], half, 1))
+                deep_send[kind, face, i] = value
+            part = (kind, face, pl.ds(0, len(firsts)))
+            copies.append(start(deep_send.at[part], deep_recv.at[part], deep_send_sem.at[kind, face],
+                                deep_recv_sem.at[kind, face], 4 + face))
+        return copies
+
+    def widen(kind, firsts, seconds):
+        results = [], []
+        for i in range(len(firsts)):
+            below, above = deep_recv[kind, 0, i], deep_recv[kind, 1, i]
+            other = jnp.where(lane < half, above, pltpu.roll(below, half, 1))
+            results[0].append(jnp.concatenate([firsts[i], other], axis=1))
+            other = jnp.where(lane < half, pltpu.roll(above, half, 1), below)
+            results[1].append(jnp.concatenate([seconds[i], other], axis=1))
+        return results
 
     def edge_lanes(minus, plus, i):
         return jnp.where(lane < lanes // 2, spread_lane(minus[:, i:i + 1]), spread_lane(plus[:, i:i + 1]))
@@ -130,8 +183,9 @@
         order_z[face] = value.astype(jnp.bfloat16)
         order_copies.append(start(order_z.at[face], order_recv_z.at[face], order_send_sem.at[4 + face],
                                   order_recv_sem.at[4 + face], 4 + face))
-    conc = [conc_ref[i] for i in range(planes)]
-    conc_copies = send_faces(0, conc)
+    own_conc = [conc_ref[i] for i in range(planes)]
+    own_rhs = [rhs_ref[i] for i in range(planes)]
+    conc_copies = send_halves(0, own_conc, own_rhs)
 
     id_lane = lax.broadcasted_iota(jnp.int32, shape, 1)
     ids_next = jnp.where(id_lane == lanes - 1, -1.0, pltpu.roll(ids_lane, lanes - 1, 1))
@@ -227,20 +281,30 @@
         total = total + jnp.where(at_edge, edge_lanes(ends[0], ends[1], i), 0.0)
         mob_ref[i] = total
         mobility.append(total)
-    copies = send_faces(1, mobility)
+    middle = planes // 2
+    copies = send_halves(1, mobility[:middle], mobility[middle:])
+    wait(conc_copies)
+    conc, rhs = widen(0, own_conc, own_rhs)
+    for i in range(planes):
+        rhs_wide[i] = rhs[i]
+    conc_copies = send_faces(0, conc, 1)
     wait(copies)
-
-    minus, plus = recv[1, 4], recv[1, 5]
+    lower, upper = widen(1, mobility[:middle], mobility[middle:])
+    mobility = lower + upper
+    copies = send_faces(1, mobility, 1)
     for i in range(planes):
         own = mobility[i]
-        rims = edge_rows(1, i)
-        tips = edge_lanes(minus, plus, i)
-        fine_k[0, i] = 0.5 * (own + (mobility[i + 1] if i < planes - 1 else recv[1, 1]))
-        fine_k[1, i] = 0.5 * (own + (mobility[i - 1] if i > 0 else recv[1, 0]))
-        fine_k[2, i] = 0.5 * (own + jnp.where(row == rows - 1, rims, pltpu.roll(own, rows - 1, 0)))
-        fine_k[3, i] = 0.5 * (own + jnp.where(row == 0, rims, pltpu.roll(own, 1, 0)))
-        fine_k[4, i] = 0.5 * (own + jnp.where(lane == lanes - 1, tips, pltpu.roll(own, lanes - 1, 1)))
-        fine_k[5, i] = 0.5 * (own + jnp.where(lane == 0, tips, pltpu.roll(own, 1, 1)))
+        fine_k[4, i] = 0.5 * (own + pltpu.roll(own, wide - 1, 1))
+        fine_k[5, i] = 0.5 * (own + pltpu.roll(own, 1, 1))
+    wait(copies)
+    faces = get_faces(1, planes, 1)
+    for i in range(planes):
+        own = mobility[i]
+        rims = edge_rows(faces, i)
+        fine_k[0, i] = 0.5 * (own + (mobility[i + 1] if i < planes - 1 else faces[1]))
+        fine_k[1, i] = 0.5 * (own + (mobility[i - 1] if i > 0 else faces[0]))
+        fine_k[2, i] = 0.5 * (own + jnp.where(wide_row == rows - 1, rims, pltpu.roll(own, rows - 1, 0)))
+        fine_k[3, i] = 0.5 * (own + jnp.where(wide_row == 0, rims, pltpu.roll(own, 1, 0)))
 
     def build(store, faces, tau, width):
         for i in range(len(faces[0])):
@@ -250,22 +314,19 @@
             scale = tau * weight
             store[0, i] = scale * k[0]
             store[1, i] = scale * k[1]
-            top, bottom = row >= rows - width, row < width
-            right, left = lane >= lanes - width, lane < width
+            top, bottom = wide_row >= rows - width, wide_row < width
             a, b = scale * k[2], scale * k[3]
             store[2, i] = jnp.where(top, 0.0, a)
             store[3, i] = jnp.where(bottom, 0.0, b)
             store[4, i] = jnp.where(top, a, jnp.where(bottom, b, 0.0))
-            a, b = scale * k[4], scale * k[5]
-            store[5, i] = jnp.where(right, 0.0, a)
-            store[6, i] = jnp.where(left, 0.0, b)
-            store[7, i] = jnp.where(right, a, jnp.where(left, b, 0.0))
-            store[8, i] = weight
-            store[9, i] = diag * (1.0 / OMEGA)
+            store[5, i] = scale * k[4]
+            store[6, i] = scale * k[5]
+            store[7, i] = weight
+            store[8, i] = diag * (1.0 / OMEGA)
 
     def swap(value, dim, width):
         size = value.shape[dim]
-        index = row if dim == 0 else lane
+        index = wide_row if dim == 0 else wide_lane
         upper = (index // width) % 2 == 1
         return upper, pltpu.roll(value, width, dim), pltpu.roll(value, size - width, dim)
 
@@ -312,25 +373,25 @@
                 total = total + store[1, i] * field[i - 1]
             total = total + store[2, i] * pltpu.roll(own, rows - width, 0)
             total = total + store[3, i] * pltpu.roll(own, width, 0)
-            total = total + store[5, i] * pltpu.roll(own, lanes - width, 1)
+            total = total + store[5, i] * pltpu.roll(own, wide - width, 1)
             total = total + store[6, i] * pltpu.roll(own, width, 1)
             totals.append(total)
         if between is not None:
             between()
         wait(copies)
-        minus, plus = recv[turn, 4], recv[turn, 5]
+        faces = get_faces(turn, count, width)
         for i in range(count):
-            total = totals[i] + store[4, i] * edge_rows(turn, i) + store[7, i] * edge_lanes(minus, plus, i)
+            total = totals[i] + store[4, i] * edge_rows(faces, i)
             if i == count - 1:
-                total = total + store[0, i] * recv[turn, 1]
+                total = total + store[0, i] * faces[1]
             if i == 0:
-                total = total + store[1, i] * recv[turn, 0]
+                total = total + store[1, i] * faces[0]
             totals[i] = total
         return totals
 
     faces0 = [[fine_k[face, i] for i in range(planes)] for face in range(6)]
     build(coeff0, faces0, TAU_FINE, 1)
-    weighted0 = [coeff0[8, i] * rhs_ref[i] for i in range(planes)]
+    weighted0 = [coeff0[7, i] * rhs_wide[i] for i in range(planes)]
     keep = 1.0 - OMEGA
     field = sweep(0, conc, weighted0, coeff0, 1, conc_copies, keep)
 
@@ -340,43 +401,42 @@
         faces1.extend(coarsen(faces0, 1))
         build(coeff1, faces1, TAU_FINE / 4.0, 2)
 
-    copies = send_faces(2, field)
+    copies = send_faces(2, field, 1)
     field = sweep(2, field, weighted0, coeff0, 1, copies, keep, build_middle)
 
     def build_low():
         build(coeff2, coarsen(faces1, 2), TAU_FINE / 16.0, 4)
 
-    copies = send_faces(3, field)
+    copies = send_faces(3, field, 1)
     added = sweep(3, field, weighted0, coeff0, 1, copies, -OMEGA, build_low)
-    source1 = restrict([added[i] * coeff0[9, i] for i in range(planes)], 1)
-    middle = planes // 2
-    weighted1 = [coeff1[8, i] * source1[i] for i in range(middle)]
+    source1 = restrict([added[i] * coeff0[8, i] for i in range(planes)], 1)
+    weighted1 = [coeff1[7, i] * source1[i] for i in range(middle)]
     error1 = weighted1
-    copies = send_faces(4, error1)
+    copies = send_faces(4, error1, 2)
     error1 = sweep(4, error1, weighted1, coeff1, 2, copies, keep)
-    copies = send_faces(5, error1)
+    copies = send_faces(5, error1, 2)
     added = sweep(5, error1, weighted1, coeff1, 2, copies, -OMEGA)
-    source2 = restrict([added[i] * coeff1[9, i] for i in range(middle)], 2)
+    source2 = restrict([added[i] * coeff1[8, i] for i in range(middle)], 2)
     low = planes // 4
-    weighted2 = [coeff2[8, i] * source2[i] for i in range(low)]
+    weighted2 = [coeff2[7, i] * source2[i] for i in range(low)]
     error2 = weighted2
     turn = 6
     for _ in range(COARSE_SWEEPS - 1):
-        copies = send_faces(turn, error2)
+        copies = send_faces(turn, error2, 4)
         error2 = sweep(turn, error2, weighted2, coeff2, 4, copies, keep)
         turn += 1
     error1 = [error1[i] + error2[i // 2] for i in range(middle)]
     for _ in range(2):
-        copies = send_faces(turn, error1)
+        copies = send_faces(turn, error1, 2)
         error1 = sweep(turn, error1, weighted1, coeff1, 2, copies, keep)
         turn += 1
     field = [field[i] + error1[i // 2] for i in range(planes)]
     for _ in range(2):
-        copies = send_faces(turn, field)
+        copies = send_faces(turn, field, 1)
         field = sweep(turn, field, weighted0, coeff0, 1, copies, keep)
         turn += 1
     for i in range(planes):
-        sol_ref[i] = field[i]
+        sol_ref[i] = field[i][:, :lanes]
     for copy in started:
         copy.wait_send()
 
@@ -386,6 +446,7 @@
 
 def body(counts, conc, right_side, order_field, grain_ids):
     planes, rows, lanes = conc.shape
+    wide = 2 * lanes
     blocks = grain_ids.shape[2]
     vmem = pl.BlockSpec(memory_space=pltpu.VMEM)
     f32, bf16 = jnp.float32, jnp.bfloat16
@@ -394,11 +455,18 @@
     return pl.pallas_call(
         functools.partial(kernel, counts),
         out_shape=(out, out),
-        in_specs=[vmem] * 4,
+        in_specs=[pl.BlockSpec(memory_space=pltpu.HBM)] * 4,
         out_specs=(vmem, vmem),
         scratch_shapes=[
-            pltpu.VMEM((TURNS, 6, rows, lanes), f32),
-            pltpu.VMEM((TURNS, 6, rows, lanes), f32),
+            pltpu.VMEM(conc.shape, f32),
+            pltpu.VMEM(conc.shape, f32),
+            pltpu.VMEM(order_field.shape, bf16),
+            pltpu.VMEM(grain_ids.shape, jnp.int32),
+            pltpu.VMEM((planes, rows, wide), f32),
+            pltpu.VMEM((2, 2, planes, rows, lanes), f32),
+            pltpu.VMEM((2, 2, planes, rows, lanes), f32),
+            pltpu.VMEM((TURNS, 4, rows, wide), f32),
+            pltpu.VMEM((TURNS, 4, rows, wide), f32),
             pltpu.VMEM((2, SLOTS, planes, lanes), bf16),
             pltpu.VMEM((2, rows, lanes), bf16),
             pltpu.VMEM((2, SLOTS, rows, lanes), bf16),
@@ -407,16 +475,19 @@
             pltpu.VMEM((2, blocks, lanes), f32),
             pltpu.VMEM((6, blocks, lanes), f32),
             pltpu.VMEM((2, SLOTS, planes, lanes), f32),
-            pltpu.VMEM((6, planes, rows, lanes), f32),
-            pltpu.VMEM((10, planes, rows, lanes), f32),
-            pltpu.VMEM((10, planes // 2, rows, lanes), f32),
-            pltpu.VMEM((10, planes // 4, rows, lanes), f32),
-            dma((TURNS, 6)),
-            dma((TURNS, 6)),
+            pltpu.VMEM((6, planes, rows, wide), f32),
+            pltpu.VMEM((9, planes, rows, wide), f32),
+            pltpu.VMEM((9, planes // 2, rows, wide), f32),
+            pltpu.VMEM((9, planes // 4, rows, wide), f32),
+            dma((TURNS, 4)),
+            dma((TURNS, 4)),
             dma((6,)),
             dma((6,)),
             dma((6,)),
             dma((6,)),
+            dma((2, 2)),
+            dma((2, 2)),
+            dma((4,)),
         ],
         compiler_params=pltpu.CompilerParams(
             collective_id=0, has_side_effects=True, vmem_limit_bytes=40 * 1024 * 1024

time: 79.5 us -> 72.2 us (0.908)
  Pallas kernels: 73.7 us -> 66.5 us
    pallas_call x1, Pallas kernels: 73.7 us -> 66.5 us  [body(): pl.pallas_call(functools.partial(kernel, counts), out_shape=(out, out), i...]
where the time goes in v2:
time: 72.2 us; the launch traced here: 72 us
  Pallas kernels  66.5 us (92%)
  local copies, waits for them, and re-layouts  4.84 us (7%)
    pallas_call x1, Pallas kernels, body(): pl.pallas_call(functools.partial(kernel, counts), out_shape=(out, out), i...  66.5 us
    unnamed x10, local copies, waits for them, and re-layouts  4.84 us

profile of v2, /device:TPU:0, one launch (start us, length us, event | category | flops | bytes accessed | tf_op | source)
XLA Modules:
  0.0 72.0 jit_solution(1743530104837179770)
XLA Ops:
  0.6 0.0 copy-start
  0.6 1.0 %copy-done = bf16[8,16,16,128]{3,2,1,0:T(8,128)(2,1)S(1)} copy-done((bf16[8,16,16,128]{3,2,1,0:T(8,128)(2,1)S(1)}, bf16[8,16,16,128]{3,2,1,0:T(8,128)(2,1)}, u32[]{:S(2)}) %copy-start) | copy-done | bytes 524312
  1.7 0.0 copy-start.1
  1.7 0.9 %copy-done.1 = f32[16,16,128]{2,1,0:T(8,128)S(1)} copy-done((f32[16,16,128]{2,1,0:T(8,128)S(1)}, f32[16,16,128]{2,1,0:T(8,128)}, u32[]{:S(2)}) %copy-start.1) | copy-done | bytes 131096
  2.6 0.0 copy-start.2
  2.6 0.9 %copy-done.2 = f32[16,16,128]{2,1,0:T(8,128)S(1)} copy-done((f32[16,16,128]{2,1,0:T(8,128)S(1)}, f32[16,16,128]{2,1,0:T(8,128)}, u32[]{:S(2)}) %copy-start.2) | copy-done | bytes 131096
  3.5 0.0 copy-start.3
  3.5 0.7 copy-done.3
  4.2 66.5 %shard_map.59 = (f32[16,16,128]{2,1,0:T(8,128)S(1)}, f32[16,16,128]{2,1,0:T(8,128)S(1)}) custom-call(f32[16,16,128]{2,1,0:T(8,128)S(1)} %copy-done.1, f32[16,16,128]{2,1,0:T(8,128)S(1)} %copy-done.2, bf16[8,16,16,128]{3,2,1,0:T(8,128)(2,1)S(1)} %copy-done, s32[1,1,8,8]{3,2,1,0:T(8,128)S(1)} %copy-done.3), custom_call_target="tpu_custom_call" | custom-call | tf_op jit(solution)/shard_map/pallas_call | solution.py:455
  70.7 0.7 copy.8
  71.4 0.7 copy.9
Async XLA Ops:
  0.6 1.0 %copy-start = (bf16[8,16,16,128]{3,2,1,0:T(8,128)(2,1)S(1)}, bf16[8,16,16,128]{3,2,1,0:T(8,128)(2,1)}, u32[]{:S(2)}) copy-start(bf16[8,16,16,128]{3,2,1,0:T(8,128)(2,1)} %order_in.1) | copy-start | bytes 1572868
  1.7 0.9 %copy-start.1 = (f32[16,16,128]{2,1,0:T(8,128)S(1)}, f32[16,16,128]{2,1,0:T(8,128)}, u32[]{:S(2)}) copy-start(f32[16,16,128]{2,1,0:T(8,128)} %conc_in.1) | copy-start | bytes 393220
  2.6 0.9 %copy-start.2 = (f32[16,16,128]{2,1,0:T(8,128)S(1)}, f32[16,16,128]{2,1,0:T(8,128)}, u32[]{:S(2)}) copy-start(f32[16,16,128]{2,1,0:T(8,128)} %rhs_in.1) | copy-start | bytes 393220
  3.5 0.7 copy-start.3

commit v3 on v2

--- a/solution.py
+++ b/solution.py
@@ -18,9 +18,10 @@
 
 
 def kernel(counts, conc_in, rhs_in, order_in, ids_in, sol_ref, mob_ref, conc_ref, rhs_ref, order_ref, ids_ref, rhs_wide,
-           deep_send, deep_recv, send, recv, order_y, order_z, order_recv_x,
+           deep_send, deep_recv, group_send, group_recv, group_dense, send, recv, order_y, order_z, order_recv_x,
            order_recv_y, order_recv_z, ids_send, ids_recv, rows_ref, fine_k, coeff0, coeff1, coeff2, send_sem,
-           recv_sem, order_send_sem, order_recv_sem, ids_send_sem, ids_recv_sem, deep_send_sem, deep_recv_sem, load_sem):
+           recv_sem, order_send_sem, order_recv_sem, ids_send_sem, ids_recv_sem, deep_send_sem, deep_recv_sem, group_send_sem,
+           group_recv_sem, load_sem):
     planes, rows, lanes = conc_ref.shape
     wide = 2 * lanes
     half = lanes // 2
@@ -41,9 +42,14 @@
     targets = [beside(dim, sign) for dim in range(3) for sign in (1, -1)]
 
     barrier = pltpu.get_barrier_semaphore()
-    for target in targets:
+    spots = [(x, y) for x in range(counts[0]) for y in range(counts[1])]
+    group = [
+        (lax.rem(me[0] - x + counts[0], counts[0]), lax.rem(me[1] - y + counts[1], counts[1]), me[2]) for x, y in spots
+    ]
+    greeted = targets[4:] + group[1:]
+    for target in greeted:
         pl.semaphore_signal(barrier, inc=1, device_id=target, device_id_type=MESH)
-    pl.semaphore_wait(barrier, 6)
+    pl.semaphore_wait(barrier, len(greeted))
     for load in loads:
         load.wait()
 
@@ -52,9 +58,9 @@
     zero = jnp.zeros((rows, lanes), jnp.float32)
     started = []
 
-    def start(source, dest, source_sem, dest_sem, face):
+    def start(source, dest, source_sem, dest_sem, face, target=None):
         copy = pltpu.make_async_remote_copy(
-            src_ref=source, dst_ref=dest, send_sem=source_sem, recv_sem=dest_sem, device_id=targets[face],
+            src_ref=source, dst_ref=dest, send_sem=source_sem, recv_sem=dest_sem, device_id=targets[face] if target is None else target,
             device_id_type=MESH)
         copy.start()
         started.append(copy)
@@ -106,11 +112,33 @@
     def get_faces(turn, count, width):
         extent = max(count, 8)
         span = pl.ds(0, wide if width == 1 else lanes)
-        return [unfold(recv[turn, face, pl.ds(0, rows if face < 2 else extent), span], width) for face in range(4)]
+        whole = [unfold(recv[turn, face, pl.ds(0, rows if face < 2 else extent), span], width) for face in range(4)]
+        return whole[:2] + [[face[i:i + 1, :] for i in range(count)] for face in whole[2:]]
 
     def edge_rows(faces, i):
-        return jnp.where(wide_row < rows // 2, jnp.broadcast_to(faces[2][i:i + 1, :], (rows, wide)),
-                         jnp.broadcast_to(faces[3][i:i + 1, :], (rows, wide)))
+        return jnp.where(wide_row < rows // 2, jnp.broadcast_to(faces[2][i], (rows, wide)),
+                         jnp.broadcast_to(faces[3][i], (rows, wide)))
+
+    low = planes // 4
+
+    def send_group(kind, field):
+        packed = field[0]
+        for i in range(1, low):
+            packed = jnp.where(wide_row % low == i, field[i], packed)
+        group_send[kind] = fold(packed, 4)
+        copies = []
+        for spot in range(1, len(spots)):
+            copies.append(start(group_send.at[kind], group_recv.at[kind, spot], group_send_sem.at[kind, spot],
+                                group_recv_sem.at[kind, spot], 0, group[spot]))
+        group_recv[kind, 0] = group_send[kind]
+        return copies
+
+    def get_group(kind):
+        for spot, (x, y) in enumerate(spots):
+            for i in range(low):
+                group_dense[kind, x * low + i, y * low:(y + 1) * low, :] = (
+                    group_recv[kind, spot, pl.ds(i, low, stride=low), :])
+        return [unfold(group_dense[kind, i], 4) for i in range(low * counts[0])]
 
     def send_halves(kind, firsts, seconds):
         copies = []
@@ -361,7 +389,7 @@
             for i in range(len(field) // 2)
         ]
 
-    def sweep(turn, field, weighted, store, width, copies, keep, between=None):
+    def sweep(turn, field, weighted, store, width, copies, keep, between=None, faces=None):
         count = len(field)
         totals = []
         for i in range(count):
@@ -379,7 +407,8 @@
         if between is not None:
             between()
         wait(copies)
-        faces = get_faces(turn, count, width)
+        if faces is None:
+            faces = get_faces(turn, count, width)
         for i in range(count):
             total = totals[i] + store[4, i] * edge_rows(faces, i)
             if i == count - 1:
@@ -404,32 +433,79 @@
     copies = send_faces(2, field, 1)
     field = sweep(2, field, weighted0, coeff0, 1, copies, keep, build_middle)
 
+    low_copies = []
+
+    def share_low():
+        low_faces = coarsen(faces1, 2)
+        for dim in range(3):
+            low_copies.extend(send_group(dim, low_faces[2 * dim]))
+
+    span = low * counts[0]
+    depth = low * counts[1]
+
     def build_low():
-        build(coeff2, coarsen(faces1, 2), TAU_FINE / 16.0, 4)
+        wait(low_copies)
+        along_x, along_y, along_z = get_group(0), get_group(1), get_group(2)
+        tau = TAU_FINE / 16.0
+        for i in range(span):
+            k = [along_x[i], along_x[i - 1], along_y[i], pltpu.roll(along_y[i], 1, 0), along_z[i],
+                 pltpu.roll(along_z[i], 4, 1)]
+            weight = OMEGA / (1.0 + tau * (k[0] + k[1] + k[2] + k[3] + k[4] + k[5]))
+            scale = tau * weight
+            for face in range(6):
+                coeff2[face, i] = scale * k[face]
+            coeff2[6, i] = weight
+
+    def low_sweep(field, weighted):
+        result = []
+        for i in range(span):
+            own = field[i]
+            total = keep * own + weighted[i]
+            total = total + coeff2[0, i] * field[(i + 1) % span]
+            total = total + coeff2[1, i] * field[i - 1]
+            total = total + coeff2[2, i] * pltpu.roll(own, depth - 1, 0)
+            total = total + coeff2[3, i] * pltpu.roll(own, 1, 0)
+            total = total + coeff2[4, i] * pltpu.roll(own, wide - 4, 1)
+            total = total + coeff2[5, i] * pltpu.roll(own, 4, 1)
+            result.append(total)
+        return result
 
     copies = send_faces(3, field, 1)
-    added = sweep(3, field, weighted0, coeff0, 1, copies, -OMEGA, build_low)
+    added = sweep(3, field, weighted0, coeff0, 1, copies, -OMEGA, share_low)
     source1 = restrict([added[i] * coeff0[8, i] for i in range(planes)], 1)
     weighted1 = [coeff1[7, i] * source1[i] for i in range(middle)]
     error1 = weighted1
     copies = send_faces(4, error1, 2)
     error1 = sweep(4, error1, weighted1, coeff1, 2, copies, keep)
     copies = send_faces(5, error1, 2)
-    added = sweep(5, error1, weighted1, coeff1, 2, copies, -OMEGA)
+    added = sweep(5, error1, weighted1, coeff1, 2, copies, -OMEGA, build_low)
     source2 = restrict([added[i] * coeff1[8, i] for i in range(middle)], 2)
-    low = planes // 4
-    weighted2 = [coeff2[7, i] * source2[i] for i in range(low)]
+    wait(send_group(3, source2))
+    source2 = get_group(3)
+    weighted2 = [coeff2[6, i] * source2[i] for i in range(span)]
     error2 = weighted2
+    for _ in range(COARSE_SWEEPS - 1):
+        error2 = low_sweep(error2, weighted2)
+
+    def spread(plane):
+        value = jnp.broadcast_to(plane[0:1, :], (rows, wide))
+        for j in range(1, low):
+            value = jnp.where(wide_row >= j * (rows // low), jnp.broadcast_to(plane[j:j + 1, :], (rows, wide)), value)
+        return value
+
+    below, above = span - 1, low % span
+    left, right = depth - 1, low % depth
+    old = get_faces(5, middle, 2)
+    faces = [old[0] + spread(error2[below]), old[1] + spread(error2[above]),
+             [old[2][i] + error2[i // 2][left:left + 1, :] for i in range(middle)],
+             [old[3][i] + error2[i // 2][right:right + 1, :] for i in range(middle)]]
+    spread2 = [spread(error2[i]) for i in range(low)]
+    error1 = [error1[i] + spread2[i // 2] for i in range(middle)]
+    error1 = sweep(5, error1, weighted1, coeff1, 2, [], keep, faces=faces)
     turn = 6
-    for _ in range(COARSE_SWEEPS - 1):
-        copies = send_faces(turn, error2, 4)
-        error2 = sweep(turn, error2, weighted2, coeff2, 4, copies, keep)
-        turn += 1
-    error1 = [error1[i] + error2[i // 2] for i in range(middle)]
-    for _ in range(2):
-        copies = send_faces(turn, error1, 2)
-        error1 = sweep(turn, error1, weighted1, coeff1, 2, copies, keep)
-        turn += 1
+    copies = send_faces(turn, error1, 2)
+    error1 = sweep(turn, error1, weighted1, coeff1, 2, copies, keep)
+    turn += 1
     field = [field[i] + error1[i // 2] for i in range(planes)]
     for _ in range(2):
         copies = send_faces(turn, field, 1)
@@ -441,7 +517,7 @@
         copy.wait_send()
 
 
-TURNS = 6 + (COARSE_SWEEPS - 1) + 4
+TURNS = 9
 
 
 def body(counts, conc, right_side, order_field, grain_ids):
@@ -465,6 +541,9 @@
             pltpu.VMEM((planes, rows, wide), f32),
             pltpu.VMEM((2, 2, planes, rows, lanes), f32),
             pltpu.VMEM((2, 2, planes, rows, lanes), f32),
+            pltpu.VMEM((4, rows, lanes), f32),
+            pltpu.VMEM((4, counts[0] * counts[1], rows, lanes), f32),
+            pltpu.VMEM((4, planes // 4 * counts[0], rows // 4 * counts[1], lanes), f32),
             pltpu.VMEM((TURNS, 4, rows, wide), f32),
             pltpu.VMEM((TURNS, 4, rows, wide), f32),
             pltpu.VMEM((2, SLOTS, planes, lanes), bf16),
@@ -478,7 +557,7 @@
             pltpu.VMEM((6, planes, rows, wide), f32),
             pltpu.VMEM((9, planes, rows, wide), f32),
             pltpu.VMEM((9, planes // 2, rows, wide), f32),
-            pltpu.VMEM((9, planes // 4, rows, wide), f32),
+            pltpu.VMEM((7, planes // 4 * counts[0], rows // 4 * counts[1], wide), f32),
             dma((TURNS, 4)),
             dma((TURNS, 4)),
             dma((6,)),
@@ -487,10 +566,12 @@
             dma((6,)),
             dma((2, 2)),
             dma((2, 2)),
+            dma((4, counts[0] * counts[1])),
+            dma((4, counts[0] * counts[1])),
             dma((4,)),
         ],
         compiler_params=pltpu.CompilerParams(
-            collective_id=0, has_side_effects=True, vmem_limit_bytes=40 * 1024 * 1024
+            collective_id=0, has_side_effects=True, vmem_limit_bytes=62 * 1024 * 1024
         ),
     )(conc, right_side, order_field, grain_ids)
 

time: 72.2 us -> 52.4 us (0.73)
  Pallas kernels: 66.5 us -> 49.3 us
  local copies, waits for them, and re-layouts: 4.84 us -> 2.26 us
    pallas_call x1, Pallas kernels: 66.5 us -> 49.3 us  [body(): pl.pallas_call(functools.partial(kernel, counts), out_shape=(out, out), i...]
    unnamed x10 -> x4, local copies, waits for them, and re-layouts: 4.84 us -> 2.26 us
where the time goes in v3:
time: 52.4 us; the launch traced here: 52.2 us
  Pallas kernels  49.3 us (94%)
  local copies, waits for them, and re-layouts  2.26 us (4%)
  between operations  0.65 us (1%)
    pallas_call x1, Pallas kernels, body(): pl.pallas_call(functools.partial(kernel, counts), out_shape=(out, out), i...  49.3 us
    unnamed x4, local copies, waits for them, and re-layouts  2.26 us

profile of v3, /device:TPU:0, one launch (start us, length us, event | category | flops | bytes accessed | tf_op | source)
XLA Modules:
  0.0 52.2 jit_solution(14038085247441432886)
XLA Ops:
  0.6 49.3 %shard_map.59 = (f32[16,16,128]{2,1,0:T(8,128)}, f32[16,16,128]{2,1,0:T(8,128)}) custom-call(f32[16,16,128]{2,1,0:T(8,128)} %conc_in.1, f32[16,16,128]{2,1,0:T(8,128)} %rhs_in.1, bf16[8,16,16,128]{3,2,1,0:T(8,128)(2,1)} %order_in.1, s32[1,1,8,8]{3,2,1,0:T(8,128)} %ids_in.1), custom_call_target="tpu_custom_call" | custom-call | tf_op jit(solution)/shard_map/pallas_call | solution.py:531
  50.0 0.0 copy-start
  50.0 1.6 %copy.8 = f32[16,16,128]{2,1,0:T(8,128)} copy(f32[16,16,128]{2,1,0:T(8,128)} %get-tuple-element.4) | data formatting | bytes 262144
  51.6 0.0 copy-done
  51.6 0.7 %copy.9 = f32[16,16,128]{2,1,0:T(8,128)} copy(f32[16,16,128]{2,1,0:T(8,128)S(1)} %copy-done) | data formatting | bytes 262144
Async XLA Ops:
  50.0 1.6 %copy-start = (f32[16,16,128]{2,1,0:T(8,128)S(1)}, f32[16,16,128]{2,1,0:T(8,128)}, u32[]{:S(2)}) copy-start(f32[16,16,128]{2,1,0:T(8,128)} %get-tuple-element.5) | copy-start | bytes 393220

commit v4 on v3

--- a/solution.py
+++ b/solution.py
@@ -18,10 +18,10 @@
 
 
 def kernel(counts, conc_in, rhs_in, order_in, ids_in, sol_ref, mob_ref, conc_ref, rhs_ref, order_ref, ids_ref, rhs_wide,
-           deep_send, deep_recv, group_send, group_recv, group_dense, send, recv, order_y, order_z, order_recv_x,
+           deep_send, deep_recv, group_send, group_recv, group_dense, corner_recv, send, recv, order_y, order_z, order_recv_x,
            order_recv_y, order_recv_z, ids_send, ids_recv, rows_ref, fine_k, coeff0, coeff1, coeff2, send_sem,
            recv_sem, order_send_sem, order_recv_sem, ids_send_sem, ids_recv_sem, deep_send_sem, deep_recv_sem, group_send_sem,
-           group_recv_sem, load_sem):
+           group_recv_sem, corner_send_sem, corner_recv_sem, load_sem):
     planes, rows, lanes = conc_ref.shape
     wide = 2 * lanes
     half = lanes // 2
@@ -46,7 +46,10 @@
     group = [
         (lax.rem(me[0] - x + counts[0], counts[0]), lax.rem(me[1] - y + counts[1], counts[1]), me[2]) for x, y in spots
     ]
-    greeted = targets[4:] + group[1:]
+    corners = [
+        (face, side, targets[face][:2] + (targets[4 + side][2],)) for face in range(4) for side in range(2)
+    ]
+    greeted = targets[4:] + group[1:] + [target for _, _, target in corners]
     for target in greeted:
         pl.semaphore_signal(barrier, inc=1, device_id=target, device_id_type=MESH)
     pl.semaphore_wait(barrier, len(greeted))
@@ -310,6 +313,19 @@
         mob_ref[i] = total
         mobility.append(total)
     middle = planes // 2
+    edge = pl.ds(0, rows), pl.ds(0, lanes)
+    send[(1, 0) + edge] = mobility[-1]
+    send[(1, 1) + edge] = mobility[0]
+    for face, at in ((2, rows - 1), (3, 0)):
+        for i in range(planes):
+            send[1, face, i:i + 1, pl.ds(0, lanes)] = mobility[i][at:at + 1, :]
+    face_copies = []
+    for face, side, target in corners:
+        face_copies.append(start(send.at[(1, face) + edge], corner_recv.at[face, side], corner_send_sem.at[face, side],
+                                 corner_recv_sem.at[face, side], 0, target))
+    for face in range(4):
+        face_copies.append(start(send.at[(1, face) + edge], recv.at[(1, face) + edge], send_sem.at[1, face],
+                                 recv_sem.at[1, face], face))
     copies = send_halves(1, mobility[:middle], mobility[middle:])
     wait(conc_copies)
     conc, rhs = widen(0, own_conc, own_rhs)
@@ -319,13 +335,16 @@
     wait(copies)
     lower, upper = widen(1, mobility[:middle], mobility[middle:])
     mobility = lower + upper
-    copies = send_faces(1, mobility, 1)
     for i in range(planes):
         own = mobility[i]
         fine_k[4, i] = 0.5 * (own + pltpu.roll(own, wide - 1, 1))
         fine_k[5, i] = 0.5 * (own + pltpu.roll(own, 1, 1))
-    wait(copies)
-    faces = get_faces(1, planes, 1)
+    wait(face_copies)
+    faces = [
+        jnp.concatenate([recv[(1, face) + edge], jnp.where(lane < half, corner_recv[face, 1], corner_recv[face, 0])],
+                        axis=1) for face in range(4)
+    ]
+    faces = faces[:2] + [[face[i:i + 1, :] for i in range(planes)] for face in faces[2:]]
     for i in range(planes):
         own = mobility[i]
         rims = edge_rows(faces, i)
@@ -544,6 +563,7 @@
             pltpu.VMEM((4, rows, lanes), f32),
             pltpu.VMEM((4, counts[0] * counts[1], rows, lanes), f32),
             pltpu.VMEM((4, planes // 4 * counts[0], rows // 4 * counts[1], lanes), f32),
+            pltpu.VMEM((4, 2, rows, lanes), f32),
             pltpu.VMEM((TURNS, 4, rows, wide), f32),
             pltpu.VMEM((TURNS, 4, rows, wide), f32),
             pltpu.VMEM((2, SLOTS, planes, lanes), bf16),
@@ -568,6 +588,8 @@
             dma((2, 2)),
             dma((4, counts[0] * counts[1])),
             dma((4, counts[0] * counts[1])),
+            dma((4, 2)),
+            dma((4, 2)),
             dma((4,)),
         ],
         compiler_params=pltpu.CompilerParams(

time: 52.4 us -> 51.3 us (0.979)
  Pallas kernels: 49.3 us -> 48.2 us
    pallas_call x1, Pallas kernels: 49.3 us -> 48.2 us  [body(): pl.pallas_call(functools.partial(kernel, counts), out_shape=(out, out), i...]
where the time goes in v4:
time: 51.3 us; the launch traced here: 51.2 us
  Pallas kernels  48.2 us (94%)
  local copies, waits for them, and re-layouts  2.26 us (4%)
  between operations  0.65 us (1%)
    pallas_call x1, Pallas kernels, body(): pl.pallas_call(functools.partial(kernel, counts), out_shape=(out, out), i...  48.2 us
    unnamed x4, local copies, waits for them, and re-layouts  2.26 us

profile of v4, /device:TPU:0, one launch (start us, length us, event | category | flops | bytes accessed | tf_op | source)
XLA Modules:
  0.0 51.2 jit_solution(2670369751058469357)
XLA Ops:
  0.6 48.2 %shard_map.59 = (f32[16,16,128]{2,1,0:T(8,128)}, f32[16,16,128]{2,1,0:T(8,128)}) custom-call(f32[16,16,128]{2,1,0:T(8,128)} %conc_in.1, f32[16,16,128]{2,1,0:T(8,128)} %rhs_in.1, bf16[8,16,16,128]{3,2,1,0:T(8,128)(2,1)} %order_in.1, s32[1,1,8,8]{3,2,1,0:T(8,128)} %ids_in.1), custom_call_target="tpu_custom_call" | custom-call | tf_op jit(solution)/shard_map/pallas_call | solution.py:550
  48.9 0.0 copy-start
  48.9 1.6 %copy.8 = f32[16,16,128]{2,1,0:T(8,128)} copy(f32[16,16,128]{2,1,0:T(8,128)} %get-tuple-element.4) | data formatting | bytes 262144
  50.5 0.0 copy-done
  50.5 0.7 %copy.9 = f32[16,16,128]{2,1,0:T(8,128)} copy(f32[16,16,128]{2,1,0:T(8,128)S(1)} %copy-done) | data formatting | bytes 262144
Async XLA Ops:
  48.9 1.6 %copy-start = (f32[16,16,128]{2,1,0:T(8,128)S(1)}, f32[16,16,128]{2,1,0:T(8,128)}, u32[]{:S(2)}) copy-start(f32[16,16,128]{2,1,0:T(8,128)} %get-tuple-element.5) | copy-start | bytes 393220
